TPU v7x, 128 devices: a whole 4x4x4 slice. The times are simulated.
128 devices in a mesh: row: 8 (over y_lo, z), col: 16 (over y_hi, x, core).
Axes of the slice: x: 4, y: 4 (y_hi: 2, y_lo: 2; y = y_hi * 2 + y_lo), z: 4, core: 2. Of those that a mesh axis runs over, the one named last changes fastest.
Arguments:
- pair: float32 [512, 512, 128], P('row', 'col'), may hold values from -6 to 6
- chain_lengths: int32 [8], replicated, may hold values from 1 to 64, 384 in all
- tri_in: bfloat16 [128, 640], replicated, may hold values from -0.5 to 0.5
- tri_out: bfloat16 [128, 128], replicated, may hold values from -0.5 to 0.5
- att_in: bfloat16 [128, 512], replicated, may hold values from -0.5 to 0.5
- att_bias: float32 [128, 4], replicated, may hold values from -6 to 6
- att_out: bfloat16 [128, 128], replicated, may hold values from -0.5 to 0.5
Outputs:
- pair_out: float32 [512, 512, 128], P('row', 'col')
Inputs may be any that keep to these rules, and one draw needn't show every extreme that they name: Chain c holds token slots c * 64 to (c + 1) * 64 - 1, of which the first chain_lengths[c] are present; the lengths sum to 384.
All inputs are finite; a program needn't handle non-finite values.
Results may differ from a plain program's by a relative error of at most 0.012.
Values may be sent and summed in bfloat16 or wider, within the bound.
A program may use at most 128 MiB of HBM per device.

v0:
```python
import jax
import jax.numpy as jnp
from jax import lax
from jax.sharding import PartitionSpec as P

H = 4
DH = 32
HD = 128
CHAINS = 8


def from_root(shard, axis, root):
    mine = lax.axis_index(axis) == root
    return lax.psum(jnp.where(mine, shard, jnp.zeros_like(shard)), axis)


def layer_norm(values):
    center = values - jnp.mean(values, axis=-1, keepdims=True)
    spread = jnp.mean(center * center, axis=-1, keepdims=True)
    return center * lax.rsqrt(spread + 1e-05)


def token_present(chain_lengths, token_count):
    slot_size = token_count // CHAINS
    tokens = jnp.arange(token_count, dtype=jnp.int32)
    owner = (tokens // slot_size)[:, None] == jnp.arange(CHAINS, dtype=jnp.int32)[None, :]
    own_length = jnp.sum(jnp.where(owner, chain_lengths[None, :], 0), axis=1)
    return (tokens % slot_size < own_length).astype(jnp.float32)


def on_device(pair, chain_lengths, tri_in, tri_out, att_in, att_bias, att_out):
    row_count, col_count, width = pair.shape
    token_count = col_count * lax.axis_size("col")
    row_start = lax.axis_index("row") * row_count
    col_start = lax.axis_index("col") * col_count
    present = token_present(chain_lengths, token_count)
    row_present = lax.dynamic_slice_in_dim(present, row_start, row_count)
    col_present = lax.dynamic_slice_in_dim(present, col_start, col_count)
    norm1 = layer_norm(pair).astype(jnp.bfloat16)
    proj = jnp.dot(norm1.reshape(-1, width), tri_in, preferred_element_type=jnp.float32)
    proj = proj.reshape(row_count, col_count, 5 * width)
    pair_mask = row_present[:, None, None] * col_present[None, :, None]
    left = (jax.nn.sigmoid(proj[..., :width]) * proj[..., width : 2 * width] * pair_mask).astype(
        jnp.bfloat16
    )
    right = (
        jax.nn.sigmoid(proj[..., 2 * width : 3 * width])
        * proj[..., 3 * width : 4 * width]
        * pair_mask
    ).astype(jnp.bfloat16)
    out_gate = jax.nn.sigmoid(proj[..., 4 * width :])
    root_row = col_start // row_count
    row_offset = col_start - root_row * row_count
    right_slab = lax.all_gather(right, "col", axis=1, tiled=True)
    right_piece = lax.dynamic_slice_in_dim(right_slab, row_offset, col_count, 0)
    right_rows = from_root(right_piece, "row", root_row)
    tri = jnp.einsum(
        "ikc,jkc->ijc",
        lax.all_gather(left, "col", axis=1, tiled=True),
        right_rows,
        preferred_element_type=jnp.float32,
    )
    tri_norm = layer_norm(tri).astype(jnp.bfloat16)
    update = jnp.dot(tri_norm.reshape(-1, width), tri_out, preferred_element_type=jnp.float32)
    pair1 = pair + out_gate * update.reshape(row_count, col_count, width)
    norm2 = layer_norm(pair1).astype(jnp.bfloat16)
    norm_flat = norm2.reshape(-1, width)
    qkvg = jnp.dot(norm_flat, att_in, preferred_element_type=jnp.float32)
    qkvg = qkvg.reshape(row_count, col_count, 4 * HD)
    query_raw = qkvg[..., :HD]
    gate_raw = qkvg[..., 3 * HD :]
    keys_local = qkvg[..., HD : 2 * HD].astype(jnp.bfloat16)
    values_local = qkvg[..., 2 * HD : 3 * HD].astype(jnp.bfloat16)
    query = (query_raw * DH ** (-0.5)).astype(jnp.bfloat16)
    gate = jax.nn.sigmoid(gate_raw)
    query_heads = query.reshape(row_count, col_count, H, DH)
    bias_flat = jnp.dot(norm_flat.astype(jnp.float32), att_bias, precision=lax.Precision.HIGHEST)
    bias_local = jnp.transpose(bias_flat.reshape(row_count, col_count, H), (2, 0, 1))
    bias_slab = lax.all_gather(bias_local, "col", axis=2, tiled=True)
    bias_piece = lax.dynamic_slice_in_dim(bias_slab, row_offset, col_count, 1)
    bias_rows = from_root(bias_piece, "row", root_row)
    key_bias = (present - 1.0) * 1000000000.0
    key_block = lax.all_gather(keys_local, "col", axis=1, tiled=True)
    span = key_block.shape[1]
    key_heads = key_block.reshape(row_count, span, H, DH)
    value_heads = lax.all_gather(values_local, "col", axis=1, tiled=True).reshape(
        row_count, span, H, DH
    )
    score = jnp.einsum(
        "ijhd,ikhd->ihjk", query_heads, key_heads, preferred_element_type=jnp.float32
    )
    score = score + bias_rows[None]
    score = score + key_bias[None, None, None, :]
    running_max = jnp.full((row_count, H, col_count), -1e30, jnp.float32)
    new_max = jnp.maximum(running_max, jnp.max(score, axis=-1))
    expo = jnp.exp(score - new_max[..., None])
    new_sum = jnp.sum(expo, axis=-1)
    contrib = jnp.einsum(
        "ihjk,ikhd->ihjd",
        expo.astype(jnp.bfloat16),
        value_heads,
        preferred_element_type=jnp.float32,
    )
    final_carry = (new_max, new_sum, contrib)
    final_max, final_sum, final_acc = final_carry
    attended = final_acc / final_sum[..., None]
    attended = jnp.transpose(attended, (0, 2, 1, 3)).reshape(row_count, col_count, HD)
    gated = (gate * attended).astype(jnp.bfloat16)
    output = jnp.dot(gated.reshape(-1, HD), att_out, preferred_element_type=jnp.float32)
    return pair1 + output.reshape(row_count, col_count, width)


def solution(mesh):
    return jax.shard_map(
        on_device,
        mesh=mesh,
        in_specs=(P("row", "col", None), P(), P(), P(), P(), P(), P()),
        out_specs=P("row", "col", None),
        check_vma=False,
    )
```

profile of v0, /device:TPU:105, one launch (start us, length us, event | category | flops | bytes accessed | tf_op | source)
XLA Modules:
  0.0 616.0 jit_solution(13525706436379832176)
XLA Ops:
  6.5 0.8 select_reduce_fusion
  7.3 0.1 dynamic_slice.13
  7.4 0.1 dynamic_slice.12
  7.5 1.6 reduce_sum.72
  9.1 1.9 multiply_reduce_fusion.2
  10.9 0.1 broadcast_multiply_fusion
  11.0 2.3 fusion.31
  13.4 2.4 copy-done.3
  15.7 1.6 fusion.17
  17.4 0.7 all-gather.7.cloned.1.call-update
  18.2 80.1 %all-gather.5.cloned.1.call-done = bf16[64,512,128]{2,1,0:T(8,128)(2,1)} async-done(((bf16[64,32,128]{2,1,0:T(8,128)(2,1)}), bf16[64,512,128]{2,1,0:T(8,128)(2,1)}) %all-gather.5.cloned.1.call-update) | async-done | bytes 8388624 | tf_op jit(solution)/shard_map/all_gather | solution.py:54
  98.3 4.5 dynamic-slice_select_fusion
  102.9 76.2 %all-gather.7.cloned.1.call-done = bf16[64,512,128]{2,1,0:T(8,128)(2,1)} async-done(((bf16[64,32,128]{2,1,0:T(8,128)(2,1)}), bf16[64,512,128]{2,1,0:T(8,128)(2,1)}) %all-gather.7.cloned.1.call-update) | async-done | bytes 8388624 | tf_op jit(solution)/shard_map/all_gather | solution.py:59
  179.2 29.2 %copy.61 = bf16[64,512,128]{0,1,2:T(8,128)(2,1)} copy(bf16[64,512,128]{2,1,0:T(8,128)(2,1)} %all-gather.7.cloned.1.call-done) | data formatting | bytes 16777216 | tf_op jit(solution)/shard_map/all_gather | solution.py:59
  208.3 74.8 %all-reduce.3.cloned.1.call-done = bf16[32,512,128]{2,1,0:T(8,128)(2,1)} async-done(((bf16[32,512,128]{2,1,0:T(8,128)(2,1)}), bf16[32,512,128]{2,1,0:T(8,128)(2,1)}) %all-reduce.3.cloned.1.call-update) | async-done | bytes 4194320 | tf_op jit(solution)/shard_map/psum | solution.py:14
  283.1 8.0 %copy.60 = bf16[32,512,128]{1,0,2:T(8,128)(2,1)} copy(bf16[32,512,128]{2,1,0:T(8,128)(2,1)} %all-reduce.3.cloned.1.call-done) | data formatting | bytes 8388608 | tf_op jit(solution)/shard_map/psum | solution.py:14
  291.1 9.7 %bitcast_reduce_fusion = (f32[64,32]{0,1:T(8,128)S(1)}, f32[128,32,64]{2,1,0:T(8,128)S(1)}) fusion(bf16[32,512,128]{1,0,2:T(8,128)(2,1)} %copy.60, bf16[64,512,128]{0,1,2:T(8,128)(2,1)} %copy.61), kind=kOutput, calls=%fused_computation.12 | convolution fusion | flops 268695552 | bytes 13639680 | tf_op jit(solution)/shard_map/ikc,jkc->ijc/dot_general | solution.py:57
  300.9 0.1 copy.62
  301.0 0.1 copy.63
  301.0 0.3 multiply_reduce_fusion
  301.4 0.1 copy.64
  301.5 1.2 multiply_convert_fusion
  302.8 2.8 copy.66
  305.6 1.7 fusion.50
  307.4 0.6 multiply_reduce_fusion.1
  308.1 2.2 convolution_bitcast_fusion
  310.3 0.1 copy.70
  310.4 27.4 %all_gather.18 = f32[4,64,512]{1,0,2:T(4,128)S(1)} all-gather(f32[4,64,32]{1,0,2:T(4,128)S(1)} %copy.70), channel_id=1, replica_groups=mesh['row'=8,'col'=16] {'col'}, dimensions={2}, use_global_device_ids=true | all-gather | bytes 557056 | tf_op jit(solution)/shard_map/all_gather | solution.py:79
  337.8 1.6 dynamic-slice_select_fusion.1
  339.5 2.6 fusion.51
  342.1 1.2 fusion.49
  343.4 0.5 all-gather.11.cloned.1.call-update
  343.9 1.4 fusion.11
  345.3 1.6 copy.67
  346.9 4.2 copy.69
  351.1 56.6 %all-reduce.5.cloned.1.call-done = f32[4,32,512]{1,0,2:T(4,128)} async-done(((f32[4,32,512]{1,0,2:T(4,128)}), f32[4,32,512]{1,0,2:T(4,128)}) %all-reduce.5.cloned.1.call-update) | async-done | bytes 262160 | tf_op jit(solution)/shard_map/psum | solution.py:14
  407.7 1.5 copy.71
  409.2 86.1 %all-gather.9.cloned.1.call-done = bf16[64,512,128]{2,1,0:T(8,128)(2,1)} async-done(((bf16[64,32,128]{2,1,0:T(8,128)(2,1)}), bf16[64,512,128]{2,1,0:T(8,128)(2,1)}) %all-gather.9.cloned.1.call-update) | async-done | bytes 8388624 | tf_op jit(solution)/shard_map/all_gather | solution.py:83
  495.4 12.0 %copy.68 = bf16[64,512,128]{1,2,0:T(8,128)(2,1)} copy(bf16[64,512,128]{2,1,0:T(8,128)(2,1)} %all-gather.9.cloned.1.call-done) | data formatting | bytes 16777216 | tf_op jit(solution)/shard_map/all_gather | solution.py:83
  507.3 5.3 fusion
  512.7 5.7 copy-done.2
  518.4 4.5 fusion.1
  522.9 53.2 %all-gather.11.cloned.1.call-done = bf16[64,512,128]{2,1,0:T(8,128)(2,1)} async-done(((bf16[64,32,128]{2,1,0:T(8,128)(2,1)}), bf16[64,512,128]{2,1,0:T(8,128)(2,1)}) %all-gather.11.cloned.1.call-update) | async-done | bytes 8388624 | tf_op jit(solution)/shard_map/all_gather | solution.py:86
  576.1 11.9 %copy.72 = bf16[64,512,128]{1,2,0:T(8,128)(2,1)} copy(bf16[64,512,128]{2,1,0:T(8,128)(2,1)} %all-gather.11.cloned.1.call-done) | data formatting | bytes 16777216 | tf_op jit(solution)/shard_map/all_gather | solution.py:86
  588.0 12.5 %bitcast_divide_fusion = f32[64,32,4,32]{3,1,2,0:T(8,128)} fusion(bf16[64,512,4,32]{1,3,2,0:T(8,128)(2,1)} %bitcast.43, f32[64,4,32,512]{3,2,1,0:T(8,128)} %copy-done.2, f32[64,4,32]{2,1,0:T(4,128)S(1)} %broadcast_maximum_fusion, f32[512]{0:T(512)S(1)} %add_multiply_fusion, f32[4,32,512]{2,1,0:T(8,128)S(1)} %copy.71, f32[64,32,4]{1,2,0:T(4,128)S(1)} %bitcast.45), kind=kOutput, calls=%fused_computation.9 | convolution fusion | flops 285474816 | bytes 26544128 | tf_op jit(solution)/shard_map/ihjk,ikhd->ihjd/dot_general | solution.py:98
  600.5 3.9 copy.73
  604.4 1.8 copy.74
  606.2 2.9 convolution_add_fusion
  (41 shorter events, 0.5 us)
Async XLA Ops:
  6.5 4.5 copy-start
  6.5 91.8 %all-gather.5.cloned.1.call-start = ((), (), s32[]{:S(2)}) async-start(), calls=%async_computation | async-start | bytes 8912896 | tf_op jit(solution)/shard_map/all_gather | solution.py:54
  13.3 2.4 copy-start.3
  17.4 161.8 %all-gather.7.cloned.1.call-start = ((), (), s32[]{:S(2)}) async-start(), calls=%async_computation.2 | async-start | bytes 8912896 | tf_op jit(solution)/shard_map/all_gather | solution.py:59
  18.1 265.0 %all-reduce.3.cloned.1.call-start = ((), (), s32[]{:S(2)}) async-start(), calls=%async_computation.1 | async-start | bytes 8388608 | tf_op jit(solution)/shard_map/psum | solution.py:14
  102.9 304.8 %all-reduce.5.cloned.1.call-start = ((), (), s32[]{:S(2)}) async-start(), calls=%async_computation.4 | async-start | bytes 2097152 | tf_op jit(solution)/shard_map/psum | solution.py:14
  291.1 14.5 %copy-start.4 = (f32[64,32,128]{2,1,0:T(8,128)S(1)}, f32[64,32,128]{2,1,0:T(8,128)}, u32[]{:S(2)}) copy-start(f32[64,32,128]{2,1,0:T(8,128)} %param.7) | copy-start | bytes 3145732
  291.1 14.5 %copy-start.9 = (bf16[128,128]{1,0:T(8,128)(2,1)S(1)}, bf16[128,128]{1,0:T(8,128)(2,1)}, u32[]{:S(2)}) copy-start(bf16[128,128]{1,0:T(8,128)(2,1)} %param.10) | copy-start | bytes 98308
  300.9 7.2 %copy-start.8 = (f32[128,4]{0,1:T(4,128)S(1)}, f32[128,4]{0,1:T(4,128)}, u32[]{:S(2)}) copy-start(f32[128,4]{0,1:T(4,128)} %param.12) | copy-start | bytes 6148
  301.5 37.9 %copy-start.7 = (bf16[128,512]{1,0:T(8,128)(2,1)S(1)}, bf16[128,512]{1,0:T(8,128)(2,1)}, u32[]{:S(2)}) copy-start(bf16[128,512]{1,0:T(8,128)(2,1)} %param.11) | copy-start | bytes 393220
  307.4 36.0 %copy-start.5 = (f32[64,32,128]{2,1,0:T(8,128)}, f32[64,32,128]{2,1,0:T(8,128)S(1)}, u32[]{:S(2)}) copy-start(f32[64,32,128]{2,1,0:T(8,128)S(1)} %get-tuple-element.12) | copy-start | bytes 3145732
  339.4 156.0 %all-gather.9.cloned.1.call-start = ((), (), s32[]{:S(2)}) async-start(), calls=%async_computation.3 | async-start | bytes 8912896 | tf_op jit(solution)/shard_map/all_gather | solution.py:83
  343.3 232.7 %all-gather.11.cloned.1.call-start = ((), (), s32[]{:S(2)}) async-start(), calls=%async_computation.5 | async-start | bytes 8912896 | tf_op jit(solution)/shard_map/all_gather | solution.py:86
  512.7 5.7 copy-start.2
  588.0 21.1 %copy-start.1 = (bf16[128,640]{1,0:T(8,128)(2,1)S(1)}, bf16[128,640]{1,0:T(8,128)(2,1)}, u32[]{:S(2)}) copy-start(bf16[128,640]{1,0:T(8,128)(2,1)} %param.9) | copy-start | bytes 491524
  600.5 5.7 copy-start.6
  600.5 5.7 copy-start.10
Sparse Core Ops, SparseCore 0:
  17.5 80.7 all-gather.4
  100.6 78.5 all-gather.6
  181.7 101.4 all-reduce.2
  339.5 68.1 all-reduce.4
  409.8 85.5 all-gather.8
  497.5 78.5 all-gather.10
where the time goes:
time: 620 us; the launch traced here: 616 us
  waiting for transfers between devices  428 us (69%)
  local copies, waits for them, and re-layouts  86.7 us (14%)
  matrix products  39.4 us (6%)
  blocking collectives  27.4 us (4%)
  other arithmetic  20.1 us (3%)
  between operations  13.7 us (2%)
    psum x2, waiting for transfers between devices, from_root(): return lax.psum(jnp.where(mine, shard, jnp.zeros_like(shard)), axis)  131 us
    all_gather x1, waiting for transfers between devices, on_device(): key_block = lax.all_gather(keys_local, 'col', axis=1, tiled=True)  86.1 us
    all_gather x1, waiting for transfers between devices, on_device(): right_slab = lax.all_gather(right, 'col', axis=1, tiled=True)  80.1 us
    all_gather x1, waiting for transfers between devices, on_device(): lax.all_gather(left, 'col', axis=1, tiled=True)  76.2 us
    all_gather x1, waiting for transfers between devices, on_device(): lax.all_gather(values_local, 'col', axis=1, tiled=True)  53.2 us
    all_gather x1, local copies, waits for them, and re-layouts, on_device(): lax.all_gather(left, 'col', axis=1, tiled=True)  29.2 us
    all_gather x1, blocking collectives, on_device(): bias_slab = lax.all_gather(bias_local, 'col', axis=2, tiled=True)  27.4 us
    dot_general x1, matrix products, on_device(): jnp.einsum('ihjk,ikhd->ihjd', expo.astype(jnp.bfloat16), value_heads, pre...  12.5 us
  transfers between devices with their start and end apart: 6, of which 6 were waited for; matrix products, arithmetic and copies ran while one was open for 11% of the time, Pallas kernels for 0%

commit v1 on v0

v1 whole, which is shorter than its diff:
```python
import jax
import jax.numpy as jnp
from jax import lax
from jax.experimental import pallas as pl
from jax.experimental.pallas import tpu as pltpu
from jax.sharding import PartitionSpec as P

H = 4
DH = 32
CHAINS = 8
BF = jnp.bfloat16
F32 = jnp.float32


def token_present(chain_lengths, token_count):
    slot_size = token_count // CHAINS
    tokens = jnp.arange(token_count, dtype=jnp.int32)
    owner = (tokens // slot_size)[:, None] == jnp.arange(CHAINS, dtype=jnp.int32)[None, :]
    own_length = jnp.sum(jnp.where(owner, chain_lengths[None, :], 0), axis=1)
    return (tokens % slot_size < own_length).astype(jnp.float32)


def layer_norm(values, axis):
    center = values - jnp.mean(values, axis=axis, keepdims=True)
    spread = jnp.mean(center * center, axis=axis, keepdims=True)
    return center * lax.rsqrt(spread + 1e-05)


def nt(a, b):
    return lax.dot_general(a, b, (((1,), (1,)), ((), ())), preferred_element_type=F32)


def tn(a, b):
    return lax.dot_general(a, b, (((0,), (0,)), ((), ())), preferred_element_type=F32)


def nn(a, b):
    return lax.dot_general(a, b, (((1,), (0,)), ((), ())), preferred_element_type=F32)


def sigmoid(x):
    return 1.0 / (1.0 + jnp.exp(-x))


def lane_group(rows):
    return lax.broadcasted_iota(jnp.int32, (rows, 128), 1) // 32


def project_kernel(pair, weights, gate_weights, mask, send, gate, scratch):
    zero = jnp.zeros((64, 128), BF)
    for k in range(32):
        norm = layer_norm(pair[:, k, :], 1).astype(BF)
        twin = jnp.concatenate(
            [jnp.concatenate([norm, zero], 1), jnp.concatenate([zero, norm], 1)], 0
        )
        both = nt(weights[...], twin)
        out = sigmoid(both[:128]) * both[128:] * mask[k : k + 1, :]
        scratch[:, k, :] = out
        gate[:, k, :] = sigmoid(nn(norm, gate_weights[...]))
    for c in range(0, 128, 8):
        send[c : c + 8] = scratch[c : c + 8].astype(BF)


def product_kernel(got, send):
    group = lane_group(16)
    for r in range(8):
        left = got[r]
        for s in range(8):
            full = tn(left, got[s])[:64]
            parts = [full[g * 16 : (g + 1) * 16] for g in range(4)]
            for half in range(2):
                start = 64 + half * 32
                out = None
                for g in range(4):
                    shift = (g * 32 - start) % 128
                    piece = parts[g] if shift == 0 else pltpu.roll(parts[g], shift, 1)
                    out = piece if out is None else jnp.where(group == g, piece, out)
                send[r * 16 + s * 2 + half] = out.astype(BF)


def update_kernel(
    got, pair, gate, tri_out, packed_weights, bias_weights,
    pair1, send, bias, gate2, scratch,
):
    for c in range(0, 128, 8):
        scratch[c : c + 8] = got[c : c + 8].astype(F32)
    for g in range(4):
        cats = []
        for lo in range(g * 4, g * 4 + 4):
            normed = layer_norm(scratch[:, lo, :], 0).astype(BF)
            update = tn(normed, tri_out[...])
            blocks = []
            for hi in range(4):
                i = hi * 16 + lo
                new = pair[i] + gate[i] * update[hi * 32 : (hi + 1) * 32]
                pair1[i] = new
                blocks.append(layer_norm(new, 1).astype(BF))
            stacked = jnp.concatenate(blocks, 0)
            parts = nt(bias_weights[...], stacked)
            for h in range(H):
                bias[h, lo : lo + 1, :] = (
                    parts[h : h + 1] + (parts[8 + h : 9 + h] + parts[16 + h : 17 + h])
                )
            cats.append(jnp.concatenate(blocks, 1))
        rows = jnp.concatenate(cats, 0)
        for t in range(4):
            for h in range(H):
                at = (t * 4 + h) * 128
                out = nn(rows, packed_weights[:, at : at + 128])
                if t == 0:
                    out = out * (DH ** (-0.5))
                if t == 3:
                    gate2[g, h] = sigmoid(out)
                else:
                    send[h * 4 + g, t] = out.astype(BF)


def bias_kernel(got, key_bias, out):
    group = lane_group(16)
    for quad in range(4):
        for hi in range(4):
            row = None
            for q in range(4):
                piece = got[quad * 4 + q]
                shift = (q * 32 - hi * 32) % 128
                piece = piece if shift == 0 else pltpu.roll(piece, shift, 1)
                row = piece if row is None else jnp.where(group == q, piece, row)
            lanes = slice(quad * 128, quad * 128 + 128)
            out[hi * 16 : hi * 16 + 16, lanes] = row + key_bias[:, lanes]


BLOCK = 128


def attend_kernel(got, bias, out):
    group = lane_group(BLOCK)
    span = BLOCK // 32
    ones = jnp.ones((512, 128), BF)

    def row(i4, _):
        at = pl.ds(pl.multiple_of(i4 * 32, 32), 32)
        keys = got[:, 1, at, :].reshape(512, 128)
        values = jnp.concatenate([got[:, 2, at, :].reshape(512, 128), ones], 1)
        for block in range(512 // BLOCK):
            query = got[block * span : (block + 1) * span, 0, at, :].reshape(BLOCK, 128)
            total = None
            for g in range(4):
                mine = jnp.where(group == g, query, jnp.zeros_like(query))
                score = nt(mine, keys) + bias[block * BLOCK : (block + 1) * BLOCK, :]
                top = jnp.max(score, axis=1, keepdims=True)
                weights = jnp.exp(score - top).astype(BF)
                summed = nn(weights, values)
                result = summed[:, :128] / summed[:, 128:]
                total = result if total is None else jnp.where(group == g, result, total)
            out[block * span : (block + 1) * span, at, :] = total.astype(BF).reshape(span, 32, 128)
        return 0

    lax.fori_loop(0, 4, row, 0)


def finish_kernel(got, gate2, pair1, out_weights, out):
    for g in range(4):
        gated = jnp.concatenate(
            [(gate2[g, h] * got[h * 4 + g].astype(F32)).astype(BF) for h in range(H)], 1
        )
        result = nn(gated, out_weights[...])
        for hi in range(4):
            at = slice(hi * 16 + g * 4, hi * 16 + g * 4 + 4)
            out[at] = pair1[at] + result[:, hi * 128 : (hi + 1) * 128].reshape(4, 32, 128)


def call(kernel, outs, *args, scratch=(), name):
    vmem = pl.BlockSpec(memory_space=pltpu.VMEM)
    single = not isinstance(outs, tuple)
    return pl.pallas_call(
        kernel,
        out_shape=outs,
        in_specs=[vmem] * len(args),
        out_specs=vmem if single else (vmem,) * len(outs),
        scratch_shapes=scratch,
        name=name,
        compiler_params=pltpu.CompilerParams(vmem_limit_bytes=48 << 20),
    )(*args)


def shape(*dims, dtype=BF):
    return jax.ShapeDtypeStruct(dims, dtype)


def on_device(pair, chain_lengths, tri_in, tri_out, att_in, att_bias, att_out):
    row_start = lax.axis_index("row") * 64
    col_start = lax.axis_index("col") * 32
    present = token_present(chain_lengths, 512)
    row_present = lax.dynamic_slice_in_dim(present, row_start, 64)
    col_present = lax.dynamic_slice_in_dim(present, col_start, 32)
    mask = col_present[:, None] * jnp.concatenate([row_present, row_present])[None, :]
    key_bias = ((present - 1.0) * 1000000000.0)[None, :]

    pg, pv, qg, qv, og = (tri_in[:, n * 128 : (n + 1) * 128] for n in range(5))
    weights = jnp.concatenate(
        [jnp.concatenate([pg.T, qg.T], 1), jnp.concatenate([pv.T, qv.T], 1)], 0
    )
    eye = jnp.eye(4, dtype=BF)
    packed = att_in.reshape(1, 128, 4, H, 1, DH) * eye.reshape(4, 1, 1, 1, 4, 1)
    packed = packed.reshape(512, 2048)
    out_weights = att_out.reshape(H, 1, DH, 1, 128) * eye.reshape(1, 4, 1, 4, 1)
    out_weights = out_weights.reshape(512, 512)
    high = lax.reduce_precision(att_bias, 8, 7)
    rest = att_bias - high
    middle = lax.reduce_precision(rest, 8, 7)
    low = rest - middle
    pad = jnp.zeros((4, 128), BF)
    bias_weights = jnp.concatenate(
        [high.T.astype(BF), pad, middle.T.astype(BF), pad, low.T.astype(BF), pad], 0
    )

    send, gate = call(
        project_kernel,
        (shape(128, 32, 128), shape(64, 32, 128, dtype=F32)),
        pair, weights, og, mask,
        scratch=[pltpu.VMEM((128, 32, 128), F32)],
        name="project",
    )
    got = lax.all_to_all(send, ("row", "col"), 0, 0, tiled=True)
    send = call(product_kernel, shape(128, 16, 128), got.reshape(8, 512, 128), name="product")
    got = lax.all_to_all(send, ("row", "col"), 0, 0, tiled=True)
    pair1, send, bias, gate2 = call(
        update_kernel,
        (
            shape(64, 32, 128, dtype=F32),
            shape(16, 3, 128, 128),
            shape(4, 16, 128, dtype=F32),
            shape(4, 4, 128, 128, dtype=F32),
        ),
        got, pair, gate, tri_out, packed, bias_weights,
        scratch=[pltpu.VMEM((128, 16, 128), F32)],
        name="update",
    )
    bias_send = jnp.broadcast_to(bias[:, None], (4, 4, 16, 128)).reshape(16, 16, 128)
    bias_got = lax.all_to_all(bias_send, "col", 0, 0, tiled=True)
    bias_rows = call(bias_kernel, shape(64, 512, dtype=F32), bias_got, key_bias, name="bias")
    bias_send = jnp.broadcast_to(bias_rows[None], (8, 64, 512))
    bias_all = lax.all_to_all(bias_send, "row", 0, 0, tiled=True)
    got = lax.all_to_all(send, "col", 0, 0, tiled=True)
    send = call(
        attend_kernel, shape(16, 128, 128), got, bias_all.reshape(512, 512), name="attend"
    )
    got = lax.all_to_all(send, "col", 0, 0, tiled=True)
    return call(
        finish_kernel,
        shape(64, 32, 128, dtype=F32),
        got, gate2, pair1, out_weights,
        name="finish",
    )


def solution(mesh):
    return jax.shard_map(
        on_device,
        mesh=mesh,
        in_specs=(P("row", "col", None), P(), P(), P(), P(), P(), P()),
        out_specs=P("row", "col", None),
        check_vma=False,
    )
```

time: 620 us -> 154 us (0.25)
  the two profiles are of different devices: /device:TPU:105 before, /device:TPU:1 now
where the time goes in v1:
time: 154 us; the launch traced here: 153 us
  blocking collectives  75.2 us (49%)
  waiting for transfers between devices  25.6 us (17%)
  Pallas kernels  25.1 us (16%)
  starting transfers between devices  13.4 us (9%)
  local copies, waits for them, and re-layouts  11.6 us (8%)
  other arithmetic  2.07 us (1%)
    all_to_all x1, blocking collectives, on_device(): got = lax.all_to_all(send, ('row', 'col'), 0, 0, tiled=True)  30.5 us
    all_to_all x1, blocking collectives, on_device(): got = lax.all_to_all(send, 'col', 0, 0, tiled=True)  27.9 us
    pallas_call x6, Pallas kernels, call(): pl.pallas_call(kernel, out_shape=outs, in_specs=[vmem] * len(args), out_s...  25.1 us
    all_to_all x1, blocking collectives, on_device(): bias_all = lax.all_to_all(bias_send, 'row', 0, 0, tiled=True)  16.8 us
    all_to_all x1, waiting for transfers between devices, on_device(): got = lax.all_to_all(send, 'col', 0, 0, tiled=True)  11 us
    all_to_all x1, waiting for transfers between devices, on_device(): bias_got = lax.all_to_all(bias_send, 'col', 0, 0, tiled=True)  7.65 us
    all_to_all x1, waiting for transfers between devices, on_device(): got = lax.all_to_all(send, ('row', 'col'), 0, 0, tiled=True)  6.88 us
    unnamed x29, local copies, waits for them, and re-layouts  5.55 us
  transfers between devices with their start and end apart: 3, of which 3 were waited for; matrix products, arithmetic and copies ran while one was open for 5% of the time, Pallas kernels for 0%

profile of v1, /device:TPU:1, one launch (start us, length us, event | category | flops | bytes accessed | tf_op | source)
XLA Modules:
  0.0 153.0 jit_solution(1545209518233311492)
XLA Ops:
  0.0 0.7 select_reduce_fusion
  0.8 0.1 dynamic_slice.7
  0.8 0.1 pad_maximum_fusion
  0.9 0.1 dynamic_slice.6
  1.0 0.8 fusion.12
  1.8 0.1 copy.26
  1.9 0.1 copy.27
  2.1 0.1 copy.28
  2.2 0.1 copy.29
  2.3 0.1 broadcast_multiply_fusion.2.mask
  2.4 0.0 copy-start
  2.4 1.2 copy-done
  3.6 4.8 %project.1 = (bf16[128,32,128]{2,1,0:T(8,128)(2,1)S(1)}, f32[64,32,128]{2,1,0:T(8,128)S(1)}) custom-call(f32[64,32,128]{2,1,0:T(8,128)S(1)} %copy-done, bf16[256,256]{1,0:T(8,128)(2,1)S(1)} %maximum_maximum_fusion.weights, bf16[128,128]{1,0:T(8,128)(2,1)S(1)} %get-tuple-element.17.gate_weights, f32[32,128]{1,0:T(8,128)S(1)} %broadcast_multiply_fusion.2.mask), custom_call_target="tpu_custom_call" | custom-call | tf_op jit(solution)/shard_map/project/pallas_call | solution.py:175
  8.4 0.0 copy-start.8
  8.5 30.5 %all_to_all.30 = bf16[128,32,128]{2,1,0:T(8,128)(2,1)S(1)} all-to-all(bf16[128,32,128]{2,1,0:T(8,128)(2,1)S(1)} %get-tuple-element.11), channel_id=1, replica_groups=mesh['row'=8,'col'=16] {'row','col'}, dimensions={0} | all-to-all | bytes 2097152 | tf_op jit(solution)/shard_map/all_to_all | solution.py:224
  39.0 3.3 %product.1 = bf16[128,16,128]{2,1,0:T(8,128)(2,1)} custom-call(bf16[8,512,128]{2,1,0:T(8,128)(2,1)S(1)} %bitcast.29), custom_call_target="tpu_custom_call" | custom-call | tf_op jit(solution)/shard_map/product/pallas_call | solution.py:175
  42.2 4.6 %all-to-all-start.1 = ((bf16[128,16,128]{2,1,0:T(8,128)(2,1)}), bf16[128,16,128]{2,1,0:T(8,128)(2,1)S(1)}, u32[]{:S(2)}, u32[]{:S(2)}) async-start(bf16[128,16,128]{2,1,0:T(8,128)(2,1)} %product.1), calls=%async_computation.1 | async-start | bytes 1048576 | tf_op jit(solution)/shard_map/all_to_all | solution.py:226
  46.9 0.0 copy-done.8
  46.9 0.1 copy.23
  47.0 0.9 broadcast_multiply_fusion
  47.9 1.7 %copy.34 = bf16[256,8,4,128]{3,1,2,0:T(8,128)(2,1)} copy(bf16[256,8,4,128]{3,2,1,0:T(4,128)(2,1)S(1)} %bitcast.31) | data formatting | bytes 4194304
  49.6 4.0 %copy.24.packed_weights = bf16[512,2048]{1,0:T(8,128)(2,1)} copy(bf16[512,2048]{0,1:T(8,128)(2,1)} %bitcast.32) | data formatting | bytes 4194304 | tf_op jit(solution)/shard_map/mul | solution.py:204
  53.6 0.0 copy-done.10
  53.6 0.1 concatenate.19.bias_weights
  53.7 6.9 %all-to-all-done.1.got = bf16[128,16,128]{2,1,0:T(8,128)(2,1)S(1)} async-done(((bf16[128,16,128]{2,1,0:T(8,128)(2,1)}), bf16[128,16,128]{2,1,0:T(8,128)(2,1)S(1)}, u32[]{:S(2)}, u32[]{:S(2)}) %all-to-all-start.1) | async-done | bytes 524320 | tf_op jit(solution)/shard_map/all_to_all | solution.py:226
  60.6 0.0 copy-done.1
  60.6 0.0 copy-done.6
  60.6 8.3 %update.1 = (f32[64,32,128]{2,1,0:T(8,128)S(1)}, bf16[16,3,128,128]{3,2,1,0:T(8,128)(2,1)}, f32[4,16,128]{2,1,0:T(8,128)S(1)}, f32[4,4,128,128]{3,2,1,0:T(8,128)S(1)}) custom-call(bf16[128,16,128]{2,1,0:T(8,128)(2,1)S(1)} %all-to-all-done.1.got, f32[64,32,128]{2,1,0:T(8,128)S(1)} %copy-done.1, f32[64,32,128]{2,1,0:T(8,128)S(1)} %get-tuple-element.12.gate, ...), custom_call_target="tpu_custom_call" | custom-call | tf_op jit(solution)/shard_map/update/pallas_call | solution.py:175
  68.9 1.0 copy-done.2
  69.9 1.0 copy-done.4
  70.8 0.7 broadcast_in_dim.21
  71.5 4.2 %all-to-all-start.3 = ((f32[16,16,128]{2,1,0:T(8,128)}), f32[16,16,128]{2,1,0:T(8,128)S(1)}, u32[]{:S(2)}, u32[]{:S(2)}) async-start(f32[16,16,128]{2,1,0:T(8,128)} %bitcast.9), calls=%async_computation.3 | async-start | bytes 262144 | tf_op jit(solution)/shard_map/all_to_all | solution.py:240
  75.7 7.6 %all-to-all-done.3.got = f32[16,16,128]{2,1,0:T(8,128)S(1)} async-done(((f32[16,16,128]{2,1,0:T(8,128)}), f32[16,16,128]{2,1,0:T(8,128)S(1)}, u32[]{:S(2)}, u32[]{:S(2)}) %all-to-all-start.3) | async-done | bytes 131104 | tf_op jit(solution)/shard_map/all_to_all | solution.py:240
  83.4 0.2 bias.1
  83.5 0.1 broadcast_in_dim.22
  83.7 16.8 %all_to_all.31 = f32[8,64,512]{2,1,0:T(8,128)S(1)} all-to-all(f32[8,64,512]{2,1,0:T(8,128)S(1)} %broadcast_in_dim.22), channel_id=1, replica_groups=mesh['row'=8,'col'=16] {'row'}, dimensions={0} | all-to-all | bytes 2097152 | tf_op jit(solution)/shard_map/all_to_all | solution.py:243
  100.4 0.0 copy-done.7
  100.4 27.9 %all_to_all.32.got = bf16[16,3,128,128]{3,2,1,0:T(8,128)(2,1)S(1)} all-to-all(bf16[16,3,128,128]{3,2,1,0:T(8,128)(2,1)S(1)} %copy-done.7), channel_id=1, replica_groups=mesh['row'=8,'col'=16] {'col'}, dimensions={0} | all-to-all | bytes 3145728 | tf_op jit(solution)/shard_map/all_to_all | solution.py:244
  128.4 7.1 %attend.1 = bf16[16,128,128]{2,1,0:T(8,128)(2,1)} custom-call(bf16[16,3,128,128]{3,2,1,0:T(8,128)(2,1)S(1)} %all_to_all.32.got, f32[512,512]{1,0:T(8,128)S(1)} %bitcast.28), custom_call_target="tpu_custom_call" | custom-call | tf_op jit(solution)/shard_map/attend/pallas_call | solution.py:175
  135.5 4.6 %all-to-all-start.5 = ((bf16[16,128,128]{2,1,0:T(8,128)(2,1)}), bf16[16,128,128]{2,1,0:T(8,128)(2,1)S(1)}, u32[]{:S(2)}, u32[]{:S(2)}) async-start(bf16[16,128,128]{2,1,0:T(8,128)(2,1)} %attend.1), calls=%async_computation.5 | async-start | bytes 1048576 | tf_op jit(solution)/shard_map/all_to_all | solution.py:248
  140.1 0.1 copy.25
  140.2 0.0 copy-done.9
  140.2 0.3 broadcast_multiply_fusion.1
  140.4 0.1 copy.35
  140.5 11.0 %all-to-all-done.5.got = bf16[16,128,128]{2,1,0:T(8,128)(2,1)S(1)} async-done(((bf16[16,128,128]{2,1,0:T(8,128)(2,1)}), bf16[16,128,128]{2,1,0:T(8,128)(2,1)S(1)}, u32[]{:S(2)}, u32[]{:S(2)}) %all-to-all-start.5) | async-done | bytes 524320 | tf_op jit(solution)/shard_map/all_to_all | solution.py:248
  151.5 0.0 copy-done.3
  151.6 0.0 copy-done.5
  151.6 1.4 finish.1
  (16 shorter events, 0.1 us)
Async XLA Ops:
  2.4 1.2 copy-start
  8.4 38.4 %copy-start.8 = (bf16[128,512]{1,0:T(8,128)(2,1)S(1)}, bf16[128,512]{1,0:T(8,128)(2,1)}, u32[]{:S(2)}) copy-start(bf16[128,512]{1,0:T(8,128)(2,1)} %param.11) | copy-start | bytes 393220
  42.2 18.4 %all-to-all-start.1 = ((bf16[128,16,128]{2,1,0:T(8,128)(2,1)}), bf16[128,16,128]{2,1,0:T(8,128)(2,1)S(1)}, u32[]{:S(2)}, u32[]{:S(2)}) async-start(bf16[128,16,128]{2,1,0:T(8,128)(2,1)} %product.1), calls=%async_computation.1 | async-start | bytes 1048576 | tf_op jit(solution)/shard_map/all_to_all | solution.py:226
  49.6 4.0 %copy-start.10 = (f32[128,4]{0,1:T(4,128)S(1)}, f32[128,4]{0,1:T(4,128)}, u32[]{:S(2)}) copy-start(f32[128,4]{0,1:T(4,128)} %param.12) | copy-start | bytes 6148
  49.6 11.0 %copy-start.1 = (f32[64,32,128]{2,1,0:T(8,128)S(1)}, f32[64,32,128]{2,1,0:T(8,128)}, u32[]{:S(2)}) copy-start(f32[64,32,128]{2,1,0:T(8,128)} %pair.3) | copy-start | bytes 3145732
  49.6 11.0 %copy-start.6 = (bf16[128,128]{1,0:T(8,128)(2,1)S(1)}, bf16[128,128]{1,0:T(8,128)(2,1)}, u32[]{:S(2)}) copy-start(bf16[128,128]{1,0:T(8,128)(2,1)} %tri_out.1) | copy-start | bytes 98308
  68.9 1.0 copy-start.2
  69.9 1.0 copy-start.4
  70.8 29.6 %copy-start.7 = (bf16[16,3,128,128]{3,2,1,0:T(8,128)(2,1)S(1)}, bf16[16,3,128,128]{3,2,1,0:T(8,128)(2,1)}, u32[]{:S(2)}) copy-start(bf16[16,3,128,128]{3,2,1,0:T(8,128)(2,1)} %get-tuple-element.13) | copy-start | bytes 4718596
  71.5 11.8 %all-to-all-start.3 = ((f32[16,16,128]{2,1,0:T(8,128)}), f32[16,16,128]{2,1,0:T(8,128)S(1)}, u32[]{:S(2)}, u32[]{:S(2)}) async-start(f32[16,16,128]{2,1,0:T(8,128)} %bitcast.9), calls=%async_computation.3 | async-start | bytes 262144 | tf_op jit(solution)/shard_map/all_to_all | solution.py:240
  128.4 11.8 %copy-start.9 = (bf16[128,128]{1,0:T(8,128)(2,1)S(1)}, bf16[128,128]{1,0:T(8,128)(2,1)}, u32[]{:S(2)}) copy-start(bf16[128,128]{1,0:T(8,128)(2,1)} %param.13) | copy-start | bytes 98308
  135.5 16.1 %copy-start.3 = (f32[64,32,128]{2,1,0:T(8,128)S(1)}, f32[64,32,128]{2,1,0:T(8,128)}, u32[]{:S(2)}) copy-start(f32[64,32,128]{2,1,0:T(8,128)} %copy-done.2) | copy-start | bytes 3145732
  135.5 16.1 %copy-start.5 = (f32[4,4,128,128]{3,2,1,0:T(8,128)S(1)}, f32[4,4,128,128]{3,2,1,0:T(8,128)}, u32[]{:S(2)}) copy-start(f32[4,4,128,128]{3,2,1,0:T(8,128)} %copy-done.4) | copy-start | bytes 3145732
  135.5 16.1 %all-to-all-start.5 = ((bf16[16,128,128]{2,1,0:T(8,128)(2,1)}), bf16[16,128,128]{2,1,0:T(8,128)(2,1)S(1)}, u32[]{:S(2)}, u32[]{:S(2)}) async-start(bf16[16,128,128]{2,1,0:T(8,128)(2,1)} %attend.1), calls=%async_computation.5 | async-start | bytes 1048576 | tf_op jit(solution)/shard_map/all_to_all | solution.py:248

commit v2 on v1

v2 whole, which is shorter than its diff:
```python
import jax
import jax.numpy as jnp
from jax import lax
from jax.experimental import pallas as pl
from jax.experimental.pallas import tpu as pltpu
from jax.sharding import PartitionSpec as P

MESH = pl.DeviceIdType.MESH
H = 4
DH = 32
ROWS = 8
COLS = 16
BF = jnp.bfloat16
F32 = jnp.float32
BLOCK = 128
TRI, BACK, QKV, BIAS_COL, BIAS_ROW, HEADS = range(6)


def layer_norm(values, axis):
    center = values - jnp.mean(values, axis=axis, keepdims=True)
    spread = jnp.mean(center * center, axis=axis, keepdims=True)
    return center * lax.rsqrt(spread + 1e-05)


def nt(a, b):
    return lax.dot_general(a, b, (((1,), (1,)), ((), ())), preferred_element_type=F32)


def tn(a, b):
    return lax.dot_general(a, b, (((0,), (0,)), ((), ())), preferred_element_type=F32)


def nn(a, b):
    return lax.dot_general(a, b, (((1,), (0,)), ((), ())), preferred_element_type=F32)


def sigmoid(x):
    return 1.0 / (1.0 + jnp.exp(-x))


def lane_group(rows):
    return lax.broadcasted_iota(jnp.int32, (rows, 128), 1) // 32


def roll(x, shift):
    return x if shift % 128 == 0 else pltpu.roll(x, shift % 128, 1)


def block_kernel(
    pair, lengths, tri_in, tri_out, att_in, att_bias, att_out, out,
    tri_send, tri_got, back_send, back_got, qkv_send, qkv_got,
    bias_send, bias_got, bias_rows, bias_all, head_send, head_got,
    wide, gate, gate2, pair1, normed2, packed, out_packed, send_sem, recv_sem,
):
    row, col = lax.axis_index("row"), lax.axis_index("col")
    me = row * COLS + col

    def anyone(t):
        return lax.rem(row + t // COLS, ROWS), lax.rem(col + lax.rem(t, COLS), COLS)

    def each(start, stop, body):
        def step(t, carry):
            body(t)
            return carry

        lax.fori_loop(start, stop, step, 0)

    def push(phase, src, dst, device):
        pltpu.make_async_remote_copy(
            src_ref=src, dst_ref=dst, send_sem=send_sem.at[phase], recv_sem=recv_sem.at[phase],
            device_id=device, device_id_type=MESH,
        ).start()

    def landed(phase, ref):
        pltpu.make_async_copy(ref, ref, recv_sem.at[phase]).wait()

    def sent(phase, ref):
        pltpu.make_async_copy(ref, ref, send_sem.at[phase]).wait()

    barrier = pltpu.get_barrier_semaphore()

    def greet(t):
        pl.semaphore_signal(barrier, inc=1, device_id=anyone(t), device_id_type=MESH)

    each(1, ROWS * COLS, greet)

    columns = [tri_in[:, n * 128 : (n + 1) * 128] for n in range(5)]
    turned = [jnp.transpose(block.astype(F32)).astype(BF) for block in columns[:4]]
    weights = jnp.concatenate(
        [
            jnp.concatenate([turned[0], turned[2]], 1),
            jnp.concatenate([turned[1], turned[3]], 1),
        ],
        0,
    )
    lane = lax.broadcasted_iota(jnp.int32, (1, 128), 1)
    row_present = (lax.rem(lane, 64) < lengths[row]).astype(F32)
    col_length = lengths[col // 2] - lax.rem(col, 2) * 32
    zero = jnp.zeros((64, 128), BF)
    for k in range(32):
        norm = layer_norm(pair[:, k, :], 1).astype(BF)
        twin = jnp.concatenate(
            [jnp.concatenate([norm, zero], 1), jnp.concatenate([zero, norm], 1)], 0
        )
        both = nt(weights, twin)
        mask = row_present * jnp.where(k < col_length, 1.0, 0.0)
        wide[:, k, :] = sigmoid(both[:128]) * both[128:] * mask
    for c in range(0, 128, 16):
        tri_send[c : c + 16] = wide[c : c + 16].astype(BF)

    pl.semaphore_wait(barrier, ROWS * COLS - 1)

    def push_tri(t):
        r, c = anyone(t)
        push(TRI, tri_send.at[r * COLS + c], tri_got.at[me], (r, c))

    each(1, ROWS * COLS, push_tri)
    tri_got[me] = tri_send[me]

    for k in range(32):
        norm = layer_norm(pair[:, k, :], 1).astype(BF)
        gate[:, k, :] = sigmoid(nn(norm, columns[4]))
    group = lane_group(128)
    for t in range(4):
        block = att_in[:, t * 128 : (t + 1) * 128].astype(F32)
        for distance in range(4):
            moved = roll(block, distance * 32)
            for h in range(H):
                g = (h + distance) % 4
                at = (t * 4 + h) * 128
                packed[g * 128 : (g + 1) * 128, at : at + 128] = jnp.where(
                    group == g, moved, 0.0
                ).astype(BF)
    out_packed[...] = jnp.zeros_like(out_packed)
    for h in range(H):
        for g in range(4):
            at = h * 128 + g * 32
            out_packed[at : at + 32, g * 128 : (g + 1) * 128] = att_out[h * 32 : (h + 1) * 32, :]
    rest = att_bias[...]
    bias_weights = []
    for _ in range(3):
        part = rest.astype(BF)
        rest = rest - part.astype(F32)
        bias_weights.append(part)

    landed(TRI, tri_got.at[pl.ds(0, ROWS * COLS - 1)])
    group = lane_group(16)

    def product(r):
        left = tri_got[pl.ds(r * COLS, COLS)].reshape(512, 128)
        for s in range(ROWS):
            full = tn(left, tri_got[s * COLS : (s + 1) * COLS].reshape(512, 128))
            parts = [full[g * 16 : (g + 1) * 16] for g in range(4)]
            for half in range(2):
                packed_rows = None
                for g in range(4):
                    piece = roll(parts[g], g * 32 - 64 - half * 32)
                    packed_rows = piece if g == 0 else jnp.where(group == g, piece, packed_rows)
                back_send[r * COLS + s * 2 + half] = packed_rows.astype(BF)

    each(0, ROWS, product)

    def push_back(t):
        r, c = anyone(t)
        push(BACK, back_send.at[r * COLS + c], back_got.at[me], (r, c))

    each(1, ROWS * COLS, push_back)
    back_got[me] = back_send[me]
    landed(BACK, back_got.at[pl.ds(0, ROWS * COLS - 1)])

    for c in range(0, 128, 16):
        wide[c : c + 16, 0:16] = back_got[c : c + 16].astype(F32)
    for g in range(4):
        cats = []
        for lo in range(g * 4, g * 4 + 4):
            update = tn(layer_norm(wide[:, lo, :], 0).astype(BF), tri_out[...])
            blocks = []
            for hi in range(4):
                i = hi * 16 + lo
                new = pair[i] + gate[i] * update[hi * 32 : (hi + 1) * 32]
                pair1[i] = new
                blocks.append(layer_norm(new, 1).astype(BF))
            stacked = jnp.concatenate(blocks, 0)
            parts = [nt(w, stacked) for w in bias_weights]
            bias = parts[0] + (parts[1] + parts[2])
            for h in range(H):
                bias_send[h, lo : lo + 1, :] = bias[h : h + 1]
            cats.append(jnp.concatenate(blocks, 1))
        normed2[g] = jnp.concatenate(cats, 0)

    def push_bias_col(t):
        c = lax.rem(col + t, COLS)
        push(BIAS_COL, bias_send.at[c // 4], bias_got.at[col], (row, c))

    each(1, COLS, push_bias_col)
    bias_got[col] = bias_send[col // 4]

    for g in range(4):
        for t in range(3):
            for h in range(H):
                at = (t * 4 + h) * 128
                block = nn(normed2[g], packed[:, at : at + 128])
                if t == 0:
                    block = block * (DH ** (-0.5))
                qkv_send[h * 4 + g, t] = block.astype(BF)

    def push_qkv(t):
        c = lax.rem(col + t, COLS)
        push(QKV, qkv_send.at[c], qkv_got.at[col], (row, c))

    each(1, COLS, push_qkv)

    landed(BIAS_COL, bias_got.at[pl.ds(0, COLS - 1)])
    for quad in range(4):
        lanes = slice(quad * 128, quad * 128 + 128)
        length = jnp.where(lane < 64, lengths[quad * 2], lengths[quad * 2 + 1])
        key_bias = jnp.where(lax.rem(lane, 64) < length, 0.0, -1000000000.0)
        for hi in range(4):
            rows = None
            for q in range(4):
                piece = roll(bias_got[quad * 4 + q], q * 32 - hi * 32)
                rows = piece if q == 0 else jnp.where(group == q, piece, rows)
            bias_rows[hi * 16 : hi * 16 + 16, lanes] = rows + key_bias

    def push_bias_row(t):
        r = lax.rem(row + t, ROWS)
        push(BIAS_ROW, bias_rows, bias_all.at[row], (r, col))

    each(1, ROWS, push_bias_row)
    bias_all[row] = bias_rows[...]
    qkv_got[col] = qkv_send[col]

    for g in range(4):
        for h in range(H):
            at = (12 + h) * 128
            gate2[g, h] = sigmoid(nn(normed2[g], packed[:, at : at + 128]))

    landed(QKV, qkv_got.at[pl.ds(0, COLS - 1)])
    landed(BIAS_ROW, bias_all.at[pl.ds(0, ROWS - 1)])

    group = lane_group(BLOCK)
    span = BLOCK // 32
    ones = jnp.ones((512, 128), BF)

    def attend(i4):
        at = pl.ds(pl.multiple_of(i4 * 32, 32), 32)
        keys = qkv_got[:, 1, at, :].reshape(512, 128)
        values = jnp.concatenate([qkv_got[:, 2, at, :].reshape(512, 128), ones], 1)
        for block in range(512 // BLOCK):
            chunk = slice(block * span, (block + 1) * span)
            query = qkv_got[chunk, 0, at, :].reshape(BLOCK, 128)
            bias = bias_all[block * BLOCK // 64 : (block + 1) * BLOCK // 64].reshape(BLOCK, 512)
            total = None
            for g in range(4):
                mine = jnp.where(group == g, query, jnp.zeros_like(query))
                score = nt(mine, keys) + bias
                top = jnp.max(score, axis=1, keepdims=True)
                summed = nn(jnp.exp(score - top).astype(BF), values)
                result = summed[:, :128] / summed[:, 128:]
                total = result if g == 0 else jnp.where(group == g, result, total)
            head_send[chunk, at, :] = total.astype(BF).reshape(span, 32, 128)

        def push_heads(t):
            c = lax.rem(col + t, COLS)
            push(HEADS, head_send.at[c, at], head_got.at[col, at], (row, c))

        each(1, COLS, push_heads)

    each(0, 4, attend)
    head_got[col] = head_send[col]
    landed(HEADS, head_got.at[pl.ds(0, COLS - 1)])

    for g in range(4):
        gated = jnp.concatenate(
            [(gate2[g, h] * head_got[h * 4 + g].astype(F32)).astype(BF) for h in range(H)], 1
        )
        result = nn(gated, out_packed[...])
        for hi in range(4):
            rows = slice(hi * 16 + g * 4, hi * 16 + g * 4 + 4)
            out[rows] = pair1[rows] + result[:, hi * 128 : (hi + 1) * 128].reshape(4, 32, 128)

    sent(TRI, tri_send.at[pl.ds(0, ROWS * COLS - 1)])
    sent(BACK, back_send.at[pl.ds(0, ROWS * COLS - 1)])
    sent(QKV, qkv_send.at[pl.ds(0, COLS - 1)])
    sent(BIAS_COL, bias_got.at[pl.ds(0, COLS - 1)])
    sent(BIAS_ROW, bias_all.at[pl.ds(0, ROWS - 1)])
    sent(HEADS, head_send.at[pl.ds(0, COLS - 1)])


def on_device(pair, chain_lengths, tri_in, tri_out, att_in, att_bias, att_out):
    vmem = pl.BlockSpec(memory_space=pltpu.VMEM)
    return pl.pallas_call(
        block_kernel,
        out_shape=jax.ShapeDtypeStruct((64, 32, 128), F32),
        in_specs=[vmem, pl.BlockSpec(memory_space=pltpu.SMEM)] + [vmem] * 5,
        out_specs=vmem,
        scratch_shapes=[
            pltpu.VMEM((128, 32, 128), BF),
            pltpu.VMEM((128, 32, 128), BF),
            pltpu.VMEM((128, 16, 128), BF),
            pltpu.VMEM((128, 16, 128), BF),
            pltpu.VMEM((16, 3, 128, 128), BF),
            pltpu.VMEM((16, 3, 128, 128), BF),
            pltpu.VMEM((4, 16, 128), F32),
            pltpu.VMEM((16, 16, 128), F32),
            pltpu.VMEM((64, 512), F32),
            pltpu.VMEM((8, 64, 512), F32),
            pltpu.VMEM((16, 128, 128), BF),
            pltpu.VMEM((16, 128, 128), BF),
            pltpu.VMEM((128, 32, 128), F32),
            pltpu.VMEM((64, 32, 128), F32),
            pltpu.VMEM((4, 4, 128, 128), F32),
            pltpu.VMEM((64, 32, 128), F32),
            pltpu.VMEM((4, 128, 512), BF),
            pltpu.VMEM((512, 2048), BF),
            pltpu.VMEM((512, 512), BF),
            pltpu.SemaphoreType.DMA((6,)),
            pltpu.SemaphoreType.DMA((6,)),
        ],
        name="pairformer",
        compiler_params=pltpu.CompilerParams(
            collective_id=0, has_side_effects=True, vmem_limit_bytes=48 << 20
        ),
    )(pair, chain_lengths, tri_in, tri_out, att_in, att_bias.T, att_out)


def solution(mesh):
    return jax.shard_map(
        on_device,
        mesh=mesh,
        in_specs=(P("row", "col", None), P(), P(), P(), P(), P(), P()),
        out_specs=P("row", "col", None),
        check_vma=False,
    )
```

time: 154 us -> 101 us (0.66)
  the two profiles are of different devices: /device:TPU:1 before, /device:TPU:105 now
where the time goes in v2:
time: 101 us; the launch traced here: 99.6 us
  Pallas kernels  92.8 us (92%)
  local copies, waits for them, and re-layouts  6.87 us (7%)
    pallas_call x1, Pallas kernels, on_device(): pl.pallas_call(block_kernel, out_shape=jax.ShapeDtypeStruct((64, 32, 128)...  92.8 us
    unnamed x15, local copies, waits for them, and re-layouts  6.87 us

profile of v2, /device:TPU:105, one launch (start us, length us, event | category | flops | bytes accessed | tf_op | source)
XLA Modules:
  0.0 99.6 jit_solution(11101490729934515232)
XLA Ops:
  0.0 0.0 copy-start.6
  0.0 0.7 copy-done.6
  0.7 0.0 copy-start
  0.7 1.2 %copy-done = f32[64,32,128]{2,1,0:T(8,128)S(1)} copy-done((f32[64,32,128]{2,1,0:T(8,128)S(1)}, f32[64,32,128]{2,1,0:T(8,128)}, u32[]{:S(2)}) %copy-start) | copy-done | bytes 1048600
  1.9 0.0 copy-start.1
  1.9 0.9 copy-done.1
  2.8 0.0 copy-start.2
  2.8 0.9 copy-done.2
  3.7 0.0 copy-start.3
  3.7 0.8 copy-done.3
  4.5 0.0 copy-start.4
  4.5 0.8 copy-done.4
  5.2 0.0 copy-start.5
  5.2 0.7 copy-done.5
  5.9 92.8 %pairformer.1 = f32[64,32,128]{2,1,0:T(8,128)S(1)} custom-call(f32[64,32,128]{2,1,0:T(8,128)S(1)} %copy-done, s32[8]{0:T(128)S(1)} %copy-done.6, bf16[128,640]{1,0:T(8,128)(2,1)S(1)} %copy-done.1, bf16[128,128]{1,0:T(8,128)(2,1)S(1)} %copy-done.3, bf16[128,512]{1,0:T(8,128)(2,1)S(1)} %copy-done.2, f32[4,128]{1,0:T(4,128)S(1)} %bitcast.1, ...), custom_call_target="tpu_custom_call" | custom-call | tf_op jit(solution)/shard_map/pairformer/pallas_call | solution.py:292
  98.7 1.0 copy.9
Async XLA Ops:
  0.0 0.7 copy-start.6
  0.7 1.2 %copy-start = (f32[64,32,128]{2,1,0:T(8,128)S(1)}, f32[64,32,128]{2,1,0:T(8,128)}, u32[]{:S(2)}) copy-start(f32[64,32,128]{2,1,0:T(8,128)} %pair.1) | copy-start | bytes 3145732
  1.9 0.9 copy-start.1
  2.8 0.9 copy-start.2
  3.7 0.8 copy-start.3
  4.5 0.8 copy-start.4
  5.2 0.7 copy-start.5

commit v3 on v2

--- a/solution.py
+++ b/solution.py
@@ -13,7 +13,7 @@
 BF = jnp.bfloat16
 F32 = jnp.float32
 BLOCK = 128
-TRI, BACK, QKV, BIAS_COL, BIAS_ROW, HEADS = range(6)
+TRI, BACK, NORM, BIAS_COL, BIAS_ROW, BIAS_TWIN, HEADS = range(7)
 
 
 def layer_norm(values, axis):
@@ -47,13 +47,26 @@
 
 
 def block_kernel(
-    pair, lengths, tri_in, tri_out, att_in, att_bias, att_out, out,
-    tri_send, tri_got, back_send, back_got, qkv_send, qkv_got,
+    lengths, pair_in, tri_in_in, tri_out_in, att_in_in, att_bias_in, att_out_in, out,
+    pair, tri_in, tri_out, att_in, att_bias, att_out,
+    tri_send, tri_got, back_send, back_got, norm_send, norm_got,
     bias_send, bias_got, bias_rows, bias_all, head_send, head_got,
-    wide, gate, gate2, pair1, normed2, packed, out_packed, send_sem, recv_sem,
+    wide, gate, gate2, pair1, packed, gate_packed, out_packed, load_sem, send_sem, recv_sem,
 ):
     row, col = lax.axis_index("row"), lax.axis_index("col")
     me = row * COLS + col
+
+    loads = [
+        pltpu.make_async_copy(src, dst, load_sem.at[n])
+        for n, (src, dst) in enumerate(
+            [
+                (pair_in, pair), (tri_in_in, tri_in), (att_in_in, att_in),
+                (att_out_in, att_out), (att_bias_in, att_bias), (tri_out_in, tri_out),
+            ]
+        )
+    ]
+    for load in loads:
+        load.start()
 
     def anyone(t):
         return lax.rem(row + t // COLS, ROWS), lax.rem(col + lax.rem(t, COLS), COLS)
@@ -84,6 +97,7 @@
 
     each(1, ROWS * COLS, greet)
 
+    loads[1].wait()
     columns = [tri_in[:, n * 128 : (n + 1) * 128] for n in range(5)]
     turned = [jnp.transpose(block.astype(F32)).astype(BF) for block in columns[:4]]
     weights = jnp.concatenate(
@@ -97,6 +111,7 @@
     row_present = (lax.rem(lane, 64) < lengths[row]).astype(F32)
     col_length = lengths[col // 2] - lax.rem(col, 2) * 32
     zero = jnp.zeros((64, 128), BF)
+    loads[0].wait()
     for k in range(32):
         norm = layer_norm(pair[:, k, :], 1).astype(BF)
         twin = jnp.concatenate(
@@ -120,22 +135,29 @@
     for k in range(32):
         norm = layer_norm(pair[:, k, :], 1).astype(BF)
         gate[:, k, :] = sigmoid(nn(norm, columns[4]))
+    for load in loads[2:]:
+        load.wait()
     group = lane_group(128)
+    mine_first = jnp.where(col // 8 == 0, 1.0, 0.0)
     for t in range(4):
         block = att_in[:, t * 128 : (t + 1) * 128].astype(F32)
-        for distance in range(4):
-            moved = roll(block, distance * 32)
-            for h in range(H):
-                g = (h + distance) % 4
-                at = (t * 4 + h) * 128
-                packed[g * 128 : (g + 1) * 128, at : at + 128] = jnp.where(
-                    group == g, moved, 0.0
-                ).astype(BF)
+        low = jnp.where(group < 2, block, 0.0)
+        high = jnp.where(group < 2, 0.0, block)
+        low_up, high_down = roll(low, 64), roll(high, 64)
+        if t == 3:
+            gate_packed[0:128, 0:128] = low.astype(BF)
+            gate_packed[128:256, 0:128] = low_up.astype(BF)
+            gate_packed[0:128, 128:256] = high_down.astype(BF)
+            gate_packed[128:256, 128:256] = high.astype(BF)
+        else:
+            at = slice(t * 128, t * 128 + 128)
+            packed[0:128, at] = jnp.where(mine_first > 0.5, low, high_down).astype(BF)
+            packed[128:256, at] = jnp.where(mine_first > 0.5, low_up, high).astype(BF)
     out_packed[...] = jnp.zeros_like(out_packed)
-    for h in range(H):
-        for g in range(4):
-            at = h * 128 + g * 32
-            out_packed[at : at + 32, g * 128 : (g + 1) * 128] = att_out[h * 32 : (h + 1) * 32, :]
+    for p in range(2):
+        for i in range(2):
+            at = p * 128 + i * 64
+            out_packed[at : at + 64, i * 128 : (i + 1) * 128] = att_out[p * 64 : p * 64 + 64, :]
     rest = att_bias[...]
     bias_weights = []
     for _ in range(3):
@@ -170,45 +192,36 @@
 
     for c in range(0, 128, 16):
         wide[c : c + 16, 0:16] = back_got[c : c + 16].astype(F32)
-    for g in range(4):
-        cats = []
-        for lo in range(g * 4, g * 4 + 4):
-            update = tn(layer_norm(wide[:, lo, :], 0).astype(BF), tri_out[...])
-            blocks = []
-            for hi in range(4):
-                i = hi * 16 + lo
-                new = pair[i] + gate[i] * update[hi * 32 : (hi + 1) * 32]
-                pair1[i] = new
-                blocks.append(layer_norm(new, 1).astype(BF))
-            stacked = jnp.concatenate(blocks, 0)
-            parts = [nt(w, stacked) for w in bias_weights]
-            bias = parts[0] + (parts[1] + parts[2])
-            for h in range(H):
-                bias_send[h, lo : lo + 1, :] = bias[h : h + 1]
-            cats.append(jnp.concatenate(blocks, 1))
-        normed2[g] = jnp.concatenate(cats, 0)
+    for lo in range(16):
+        update = tn(layer_norm(wide[:, lo, :], 0).astype(BF), tri_out[...])
+        blocks = []
+        for hi in range(4):
+            i = hi * 16 + lo
+            new = pair[i] + gate[i] * update[hi * 32 : (hi + 1) * 32]
+            pair1[i] = new
+            block = layer_norm(new, 1).astype(BF)
+            at = (lo % 2) * 64 + (hi // 2) * 32
+            norm_send[lo // 2, at : at + 32, (hi % 2) * 128 : (hi % 2) * 128 + 128] = block
+            blocks.append(block)
+        stacked = jnp.concatenate(blocks, 0)
+        parts = [nt(w, stacked) for w in bias_weights]
+        bias = parts[0] + (parts[1] + parts[2])
+        for h in range(H):
+            bias_send[h, lo : lo + 1, :] = bias[h : h + 1]
 
     def push_bias_col(t):
         c = lax.rem(col + t, COLS)
-        push(BIAS_COL, bias_send.at[c // 4], bias_got.at[col], (row, c))
+        push(BIAS_COL, bias_send.at[c // 8 * 2 + lax.rem(c, 2)], bias_got.at[col], (row, c))
 
     each(1, COLS, push_bias_col)
-    bias_got[col] = bias_send[col // 4]
-
-    for g in range(4):
-        for t in range(3):
-            for h in range(H):
-                at = (t * 4 + h) * 128
-                block = nn(normed2[g], packed[:, at : at + 128])
-                if t == 0:
-                    block = block * (DH ** (-0.5))
-                qkv_send[h * 4 + g, t] = block.astype(BF)
-
-    def push_qkv(t):
+    head = lax.rem(col, 2)
+    bias_got[col] = bias_send[col // 8 * 2 + head]
+
+    def push_norm(t):
         c = lax.rem(col + t, COLS)
-        push(QKV, qkv_send.at[c], qkv_got.at[col], (row, c))
-
-    each(1, COLS, push_qkv)
+        push(NORM, norm_send.at[lax.rem(c, 8)], norm_got.at[col], (row, c))
+
+    each(1, COLS, push_norm)
 
     landed(BIAS_COL, bias_got.at[pl.ds(0, COLS - 1)])
     for quad in range(4):
@@ -224,36 +237,37 @@
 
     def push_bias_row(t):
         r = lax.rem(row + t, ROWS)
-        push(BIAS_ROW, bias_rows, bias_all.at[row], (r, col))
+        push(BIAS_ROW, bias_rows, bias_all.at[head, row], (r, col))
 
     each(1, ROWS, push_bias_row)
-    bias_all[row] = bias_rows[...]
-    qkv_got[col] = qkv_send[col]
-
-    for g in range(4):
-        for h in range(H):
-            at = (12 + h) * 128
-            gate2[g, h] = sigmoid(nn(normed2[g], packed[:, at : at + 128]))
-
-    landed(QKV, qkv_got.at[pl.ds(0, COLS - 1)])
-    landed(BIAS_ROW, bias_all.at[pl.ds(0, ROWS - 1)])
-
+    bias_all[head, row] = bias_rows[...]
+    norm_got[col] = norm_send[lax.rem(col, 8)]
+
+    for g in range(8):
+        gate2[g] = sigmoid(nn(norm_send[g], gate_packed[...]))
+
+    landed(BIAS_ROW, bias_all.at[0, pl.ds(0, ROWS - 1)])
+    push(BIAS_TWIN, bias_all.at[head], bias_all.at[head], (row, col + 1 - 2 * head))
+    landed(NORM, norm_got.at[pl.ds(0, COLS - 1)])
+    landed(BIAS_TWIN, bias_all.at[0])
     group = lane_group(BLOCK)
     span = BLOCK // 32
     ones = jnp.ones((512, 128), BF)
 
     def attend(i4):
         at = pl.ds(pl.multiple_of(i4 * 32, 32), 32)
-        keys = qkv_got[:, 1, at, :].reshape(512, 128)
-        values = jnp.concatenate([qkv_got[:, 2, at, :].reshape(512, 128), ones], 1)
+        normed = norm_got[:, at, :].reshape(512, 256)
+        queries = (nn(normed, packed[:, 0:128]) * (DH ** (-0.5))).astype(BF)
+        keys = nn(normed, packed[:, 128:256]).astype(BF)
+        values = jnp.concatenate([nn(normed, packed[:, 256:384]).astype(BF), ones], 1)
         for block in range(512 // BLOCK):
             chunk = slice(block * span, (block + 1) * span)
-            query = qkv_got[chunk, 0, at, :].reshape(BLOCK, 128)
-            bias = bias_all[block * BLOCK // 64 : (block + 1) * BLOCK // 64].reshape(BLOCK, 512)
+            query = queries[block * BLOCK : (block + 1) * BLOCK]
+            rows = slice(block * BLOCK // 64, (block + 1) * BLOCK // 64)
             total = None
             for g in range(4):
                 mine = jnp.where(group == g, query, jnp.zeros_like(query))
-                score = nt(mine, keys) + bias
+                score = nt(mine, keys) + bias_all[g % 2, rows].reshape(BLOCK, 512)
                 top = jnp.max(score, axis=1, keepdims=True)
                 summed = nn(jnp.exp(score - top).astype(BF), values)
                 result = summed[:, :128] / summed[:, 128:]
@@ -270,20 +284,22 @@
     head_got[col] = head_send[col]
     landed(HEADS, head_got.at[pl.ds(0, COLS - 1)])
 
-    for g in range(4):
-        gated = jnp.concatenate(
-            [(gate2[g, h] * head_got[h * 4 + g].astype(F32)).astype(BF) for h in range(H)], 1
-        )
-        result = nn(gated, out_packed[...])
-        for hi in range(4):
-            rows = slice(hi * 16 + g * 4, hi * 16 + g * 4 + 4)
-            out[rows] = pair1[rows] + result[:, hi * 128 : (hi + 1) * 128].reshape(4, 32, 128)
+    for g in range(8):
+        heads = jnp.concatenate([head_got[g], head_got[8 + g]], 1).astype(F32)
+        result = nn((gate2[g] * heads).astype(BF), out_packed[...])
+        for l in range(2):
+            for hi in range(4):
+                i = hi * 16 + g * 2 + l
+                at = l * 64 + (hi // 2) * 32
+                lanes = slice((hi % 2) * 128, (hi % 2) * 128 + 128)
+                out[i] = pair1[i] + result[at : at + 32, lanes]
 
     sent(TRI, tri_send.at[pl.ds(0, ROWS * COLS - 1)])
     sent(BACK, back_send.at[pl.ds(0, ROWS * COLS - 1)])
-    sent(QKV, qkv_send.at[pl.ds(0, COLS - 1)])
+    sent(NORM, norm_got.at[pl.ds(0, COLS - 1)])
     sent(BIAS_COL, bias_got.at[pl.ds(0, COLS - 1)])
-    sent(BIAS_ROW, bias_all.at[pl.ds(0, ROWS - 1)])
+    sent(BIAS_ROW, bias_all.at[0, pl.ds(0, ROWS - 1)])
+    sent(BIAS_TWIN, bias_all.at[0])
     sent(HEADS, head_send.at[pl.ds(0, COLS - 1)])
 
 
@@ -292,36 +308,43 @@
     return pl.pallas_call(
         block_kernel,
         out_shape=jax.ShapeDtypeStruct((64, 32, 128), F32),
-        in_specs=[vmem, pl.BlockSpec(memory_space=pltpu.SMEM)] + [vmem] * 5,
+        in_specs=[pl.BlockSpec(memory_space=pltpu.SMEM)] + [pl.BlockSpec(memory_space=pltpu.HBM)] * 6,
         out_specs=vmem,
         scratch_shapes=[
+            pltpu.VMEM((64, 32, 128), F32),
+            pltpu.VMEM((128, 640), BF),
+            pltpu.VMEM((128, 128), BF),
+            pltpu.VMEM((128, 512), BF),
+            pltpu.VMEM((4, 128), F32),
+            pltpu.VMEM((128, 128), BF),
             pltpu.VMEM((128, 32, 128), BF),
             pltpu.VMEM((128, 32, 128), BF),
             pltpu.VMEM((128, 16, 128), BF),
             pltpu.VMEM((128, 16, 128), BF),
-            pltpu.VMEM((16, 3, 128, 128), BF),
-            pltpu.VMEM((16, 3, 128, 128), BF),
+            pltpu.VMEM((8, 128, 256), BF),
+            pltpu.VMEM((16, 128, 256), BF),
             pltpu.VMEM((4, 16, 128), F32),
             pltpu.VMEM((16, 16, 128), F32),
             pltpu.VMEM((64, 512), F32),
-            pltpu.VMEM((8, 64, 512), F32),
+            pltpu.VMEM((2, 8, 64, 512), F32),
             pltpu.VMEM((16, 128, 128), BF),
             pltpu.VMEM((16, 128, 128), BF),
             pltpu.VMEM((128, 32, 128), F32),
             pltpu.VMEM((64, 32, 128), F32),
-            pltpu.VMEM((4, 4, 128, 128), F32),
+            pltpu.VMEM((8, 128, 256), F32),
             pltpu.VMEM((64, 32, 128), F32),
-            pltpu.VMEM((4, 128, 512), BF),
-            pltpu.VMEM((512, 2048), BF),
-            pltpu.VMEM((512, 512), BF),
+            pltpu.VMEM((256, 384), BF),
+            pltpu.VMEM((256, 256), BF),
+            pltpu.VMEM((256, 256), BF),
             pltpu.SemaphoreType.DMA((6,)),
-            pltpu.SemaphoreType.DMA((6,)),
+            pltpu.SemaphoreType.DMA((7,)),
+            pltpu.SemaphoreType.DMA((7,)),
         ],
         name="pairformer",
         compiler_params=pltpu.CompilerParams(
-            collective_id=0, has_side_effects=True, vmem_limit_bytes=48 << 20
+            collective_id=0, has_side_effects=True, vmem_limit_bytes=63 << 20
         ),
-    )(pair, chain_lengths, tri_in, tri_out, att_in, att_bias.T, att_out)
+    )(chain_lengths, pair, tri_in, tri_out, att_in, att_bias.T, att_out)
 
 
 def solution(mesh):

time: 101 us -> 94.7 us (0.938)
  local copies, waits for them, and re-layouts: 6.87 us -> 2.26 us
  Pallas kernels: 92.8 us -> 91.6 us
    unnamed x15 -> x1, local copies, waits for them, and re-layouts: 6.87 us -> 2.26 us
    pallas_call x1, Pallas kernels: 92.8 us -> 91.6 us  [on_device(): pl.pallas_call(block_kernel, out_shape=jax.ShapeDtypeStruct((64, 32, 128)...]
where the time goes in v3:
time: 94.7 us; the launch traced here: 93.9 us
  Pallas kernels  91.6 us (97%)
  local copies, waits for them, and re-layouts  2.26 us (2%)
    pallas_call x1, Pallas kernels, on_device(): pl.pallas_call(block_kernel, out_shape=jax.ShapeDtypeStruct((64, 32, 128)...  91.6 us
    unnamed x1, local copies, waits for them, and re-layouts  2.26 us

profile of v3, /device:TPU:105, one launch (start us, length us, event | category | flops | bytes accessed | tf_op | source)
XLA Modules:
  0.0 93.9 jit_solution(260113356786158635)
XLA Ops:
  0.0 91.6 %pairformer.1 = f32[64,32,128]{2,1,0:T(8,128)} custom-call(s32[8]{0:T(128)} %lengths.1, f32[64,32,128]{2,1,0:T(8,128)} %pair_in.1, bf16[128,640]{1,0:T(8,128)(2,1)} %tri_in_in.1, bf16[128,128]{1,0:T(8,128)(2,1)} %tri_out_in.1, bf16[128,512]{1,0:T(8,128)(2,1)} %att_in_in.1, f32[4,128]{1,0:T(4,128)} %bitcast.1, bf16[128,128]{1,0:T(8,128)(2,1)} %att_out_in.1), custom_call_target="tpu_custom_call" | custom-call | tf_op jit(solution)/shard_map/pairformer/pallas_call | solution.py:308
  91.6 2.3 %copy.9 = f32[64,32,128]{2,1,0:T(8,128)} copy(f32[64,32,128]{2,1,0:T(8,128)} %pairformer.1) | data formatting | bytes 2097152

commit v4 on v3

--- a/solution.py
+++ b/solution.py
@@ -12,7 +12,6 @@
 COLS = 16
 BF = jnp.bfloat16
 F32 = jnp.float32
-BLOCK = 128
 TRI, BACK, NORM, BIAS_COL, BIAS_ROW, BIAS_TWIN, HEADS = range(7)
 
 
@@ -51,7 +50,7 @@
     pair, tri_in, tri_out, att_in, att_bias, att_out,
     tri_send, tri_got, back_send, back_got, norm_send, norm_got,
     bias_send, bias_got, bias_rows, bias_all, head_send, head_got,
-    wide, gate, gate2, pair1, packed, gate_packed, out_packed, load_sem, send_sem, recv_sem,
+    queries, keys, values, wide, gate, gate2, pair1, packed, gate_packed, out_packed, load_sem, send_sem, recv_sem, row_sem, twin_sem,
 ):
     row, col = lax.axis_index("row"), lax.axis_index("col")
     me = row * COLS + col
@@ -78,9 +77,10 @@
 
         lax.fori_loop(start, stop, step, 0)
 
-    def push(phase, src, dst, device):
+    def push(phase, src, dst, device, arrival=None):
         pltpu.make_async_remote_copy(
-            src_ref=src, dst_ref=dst, send_sem=send_sem.at[phase], recv_sem=recv_sem.at[phase],
+            src_ref=src, dst_ref=dst, send_sem=send_sem.at[phase],
+            recv_sem=recv_sem.at[phase] if arrival is None else arrival,
             device_id=device, device_id_type=MESH,
         ).start()
 
@@ -221,66 +221,95 @@
         c = lax.rem(col + t, COLS)
         push(NORM, norm_send.at[lax.rem(c, 8)], norm_got.at[col], (row, c))
 
-    each(1, COLS, push_norm)
+    each(1, 5, push_norm)
 
     landed(BIAS_COL, bias_got.at[pl.ds(0, COLS - 1)])
-    for quad in range(4):
-        lanes = slice(quad * 128, quad * 128 + 128)
-        length = jnp.where(lane < 64, lengths[quad * 2], lengths[quad * 2 + 1])
-        key_bias = jnp.where(lax.rem(lane, 64) < length, 0.0, -1000000000.0)
-        for hi in range(4):
+    for hi in range(4):
+        quads = []
+        for quad in range(4):
             rows = None
             for q in range(4):
                 piece = roll(bias_got[quad * 4 + q], q * 32 - hi * 32)
                 rows = piece if q == 0 else jnp.where(group == q, piece, rows)
-            bias_rows[hi * 16 : hi * 16 + 16, lanes] = rows + key_bias
+            length = jnp.where(lane < 64, lengths[quad * 2], lengths[quad * 2 + 1])
+            quads.append(jnp.where(lax.rem(lane, 64) < length, rows, -1000000000.0))
+        rows = jnp.concatenate(quads, 1)
+        top = jnp.max(rows, axis=1, keepdims=True)
+        bias_rows[hi * 16 : hi * 16 + 16] = (rows - top).astype(BF)
+    bias_all[head, row] = bias_rows[...]
 
     def push_bias_row(t):
         r = lax.rem(row + t, ROWS)
-        push(BIAS_ROW, bias_rows, bias_all.at[head, row], (r, col))
-
-    each(1, ROWS, push_bias_row)
-    bias_all[head, row] = bias_rows[...]
+        push(BIAS_ROW, bias_rows, bias_all.at[head, row], (r, col), row_sem.at[row])
+
+    def push_twin(r):
+        twin = bias_all.at[head, r]
+        push(BIAS_TWIN, twin, twin, (row, col + 1 - 2 * head), twin_sem.at[r])
+
+    push_twin(row)
+
+    def push_both(t):
+        push_bias_row(t)
+        push_norm(2 * t + 3)
+        push_norm(2 * t + 4)
+
+    each(1, 6, push_both)
+    push_bias_row(6)
+    push_norm(15)
+    push_bias_row(7)
     norm_got[col] = norm_send[lax.rem(col, 8)]
 
     for g in range(8):
         gate2[g] = sigmoid(nn(norm_send[g], gate_packed[...]))
 
-    landed(BIAS_ROW, bias_all.at[0, pl.ds(0, ROWS - 1)])
-    push(BIAS_TWIN, bias_all.at[head], bias_all.at[head], (row, col + 1 - 2 * head))
     landed(NORM, norm_got.at[pl.ds(0, COLS - 1)])
-    landed(BIAS_TWIN, bias_all.at[0])
-    group = lane_group(BLOCK)
-    span = BLOCK // 32
     ones = jnp.ones((512, 128), BF)
-
-    def attend(i4):
-        at = pl.ds(pl.multiple_of(i4 * 32, 32), 32)
-        normed = norm_got[:, at, :].reshape(512, 256)
-        queries = (nn(normed, packed[:, 0:128]) * (DH ** (-0.5))).astype(BF)
-        keys = nn(normed, packed[:, 128:256]).astype(BF)
-        values = jnp.concatenate([nn(normed, packed[:, 256:384]).astype(BF), ones], 1)
-        for block in range(512 // BLOCK):
-            chunk = slice(block * span, (block + 1) * span)
-            query = queries[block * BLOCK : (block + 1) * BLOCK]
-            rows = slice(block * BLOCK // 64, (block + 1) * BLOCK // 64)
-            total = None
-            for g in range(4):
-                mine = jnp.where(group == g, query, jnp.zeros_like(query))
-                score = nt(mine, keys) + bias_all[g % 2, rows].reshape(BLOCK, 512)
-                top = jnp.max(score, axis=1, keepdims=True)
-                summed = nn(jnp.exp(score - top).astype(BF), values)
-                result = summed[:, :128] / summed[:, 128:]
-                total = result if g == 0 else jnp.where(group == g, result, total)
-            head_send[chunk, at, :] = total.astype(BF).reshape(span, 32, 128)
-
-        def push_heads(t):
-            c = lax.rem(col + t, COLS)
-            push(HEADS, head_send.at[c, at], head_got.at[col, at], (row, c))
-
-        each(1, COLS, push_heads)
-
-    each(0, 4, attend)
+    for n in range(4):
+        normed = norm_got[:, n * 32 : n * 32 + 32, :].reshape(512, 256)
+        queries[n] = (nn(normed, packed[:, 0:128]) * (DH ** (-0.5))).astype(BF)
+        keys[n] = nn(normed, packed[:, 128:256]).astype(BF)
+        values[n, :, 0:128] = nn(normed, packed[:, 256:384]).astype(BF)
+        values[n, :, 128:256] = ones
+
+    group = lane_group(64)
+
+    def attend(r):
+        pltpu.make_async_copy(bias_rows, bias_rows, twin_sem.at[r]).wait()
+        at = pl.ds(pl.multiple_of(r * 64, 64), 64)
+
+        def pair_of_rows(n):
+            query = queries[n, at, :]
+            mine = [jnp.where(group == g, query, jnp.zeros_like(query)) for g in range(4)]
+            bias = [bias_all[0, r].astype(F32), bias_all[1, r].astype(F32)]
+            score = nt(jnp.concatenate(mine, 0), keys[n]) + jnp.concatenate(bias + bias, 0)
+            top = jnp.max(score, axis=1, keepdims=True)
+            summed = nn(jnp.exp(score - top).astype(BF), values[n])
+            result = summed[:, :128] / summed[:, 128:]
+            total = result[0:64]
+            for g in range(1, 4):
+                total = jnp.where(group == g, result[g * 64 : g * 64 + 64], total)
+            to = slice(n * 32, n * 32 + 32)
+            head_send[2 * r, to, :] = total[:32].astype(BF)
+            head_send[2 * r + 1, to, :] = total[32:].astype(BF)
+
+        for n in range(4):
+            pair_of_rows(n)
+        for c in (2 * r, 2 * r + 1):
+
+            @pl.when(c != col)
+            def _():
+                push(HEADS, head_send.at[c], head_got.at[col], (row, c))
+
+    def attend_previous(t):
+        @pl.when(t < ROWS)
+        def _():
+            r = lax.rem(row - t + ROWS, ROWS)
+            pltpu.make_async_copy(bias_rows, bias_rows, row_sem.at[r]).wait()
+            push_twin(r)
+
+        attend(lax.rem(row - t + 1 + ROWS, ROWS))
+
+    each(1, ROWS + 1, attend_previous)
     head_got[col] = head_send[col]
     landed(HEADS, head_got.at[pl.ds(0, COLS - 1)])
 
@@ -325,10 +354,13 @@
             pltpu.VMEM((16, 128, 256), BF),
             pltpu.VMEM((4, 16, 128), F32),
             pltpu.VMEM((16, 16, 128), F32),
-            pltpu.VMEM((64, 512), F32),
-            pltpu.VMEM((2, 8, 64, 512), F32),
+            pltpu.VMEM((64, 512), BF),
+            pltpu.VMEM((2, 8, 64, 512), BF),
             pltpu.VMEM((16, 128, 128), BF),
             pltpu.VMEM((16, 128, 128), BF),
+            pltpu.VMEM((4, 512, 128), BF),
+            pltpu.VMEM((4, 512, 128), BF),
+            pltpu.VMEM((4, 512, 256), BF),
             pltpu.VMEM((128, 32, 128), F32),
             pltpu.VMEM((64, 32, 128), F32),
             pltpu.VMEM((8, 128, 256), F32),
@@ -339,6 +371,8 @@
             pltpu.SemaphoreType.DMA((6,)),
             pltpu.SemaphoreType.DMA((7,)),
             pltpu.SemaphoreType.DMA((7,)),
+            pltpu.SemaphoreType.DMA((8,)),
+            pltpu.SemaphoreType.DMA((8,)),
         ],
         name="pairformer",
         compiler_params=pltpu.CompilerParams(

time: 94.7 us -> 87.5 us (0.924)
  Pallas kernels: 91.6 us -> 85 us
    pallas_call x1, Pallas kernels: 91.6 us -> 85 us  [on_device(): pl.pallas_call(block_kernel, out_shape=jax.ShapeDtypeStruct((64, 32, 128)...]
where the time goes in v4:
time: 87.5 us; the launch traced here: 87.3 us
  Pallas kernels  85 us (97%)
  local copies, waits for them, and re-layouts  2.26 us (3%)
    pallas_call x1, Pallas kernels, on_device(): pl.pallas_call(block_kernel, out_shape=jax.ShapeDtypeStruct((64, 32, 128)...  85 us
    unnamed x1, local copies, waits for them, and re-layouts  2.26 us

profile of v4, /device:TPU:105, one launch (start us, length us, event | category | flops | bytes accessed | tf_op | source)
XLA Modules:
  0.0 87.3 jit_solution(12477013684429142620)
XLA Ops:
  0.0 85.0 %pairformer.1 = f32[64,32,128]{2,1,0:T(8,128)} custom-call(s32[8]{0:T(128)} %lengths.1, f32[64,32,128]{2,1,0:T(8,128)} %pair_in.1, bf16[128,640]{1,0:T(8,128)(2,1)} %tri_in_in.1, bf16[128,128]{1,0:T(8,128)(2,1)} %tri_out_in.1, bf16[128,512]{1,0:T(8,128)(2,1)} %att_in_in.1, f32[4,128]{1,0:T(4,128)} %bitcast.1, bf16[128,128]{1,0:T(8,128)(2,1)} %att_out_in.1), custom_call_target="tpu_custom_call" | custom-call | tf_op jit(solution)/shard_map/pairformer/pallas_call | solution.py:337
  85.0 2.3 %copy.9 = f32[64,32,128]{2,1,0:T(8,128)} copy(f32[64,32,128]{2,1,0:T(8,128)} %pairformer.1) | data formatting | bytes 2097152

commit v5 on v4

--- a/solution.py
+++ b/solution.py
@@ -50,7 +50,7 @@
     pair, tri_in, tri_out, att_in, att_bias, att_out,
     tri_send, tri_got, back_send, back_got, norm_send, norm_got,
     bias_send, bias_got, bias_rows, bias_all, head_send, head_got,
-    queries, keys, values, wide, gate, gate2, pair1, packed, gate_packed, out_packed, load_sem, send_sem, recv_sem, row_sem, twin_sem,
+    turned_left, queries, keys, values, wide, gate, gate2, pair1, packed, gate_packed, out_packed, load_sem, send_sem, recv_sem, tri_sem, row_sem, twin_sem,
 ):
     row, col = lax.axis_index("row"), lax.axis_index("col")
     me = row * COLS + col
@@ -127,7 +127,7 @@
 
     def push_tri(t):
         r, c = anyone(t)
-        push(TRI, tri_send.at[r * COLS + c], tri_got.at[me], (r, c))
+        push(TRI, tri_send.at[r * COLS + c], tri_got.at[me], (r, c), tri_sem.at[row])
 
     each(1, ROWS * COLS, push_tri)
     tri_got[me] = tri_send[me]
@@ -165,28 +165,47 @@
         rest = rest - part.astype(F32)
         bias_weights.append(part)
 
-    landed(TRI, tri_got.at[pl.ds(0, ROWS * COLS - 1)])
     group = lane_group(16)
 
-    def product(r):
-        left = tri_got[pl.ds(r * COLS, COLS)].reshape(512, 128)
-        for s in range(ROWS):
-            full = tn(left, tri_got[s * COLS : (s + 1) * COLS].reshape(512, 128))
-            parts = [full[g * 16 : (g + 1) * 16] for g in range(4)]
-            for half in range(2):
-                packed_rows = None
-                for g in range(4):
-                    piece = roll(parts[g], g * 32 - 64 - half * 32)
-                    packed_rows = piece if g == 0 else jnp.where(group == g, piece, packed_rows)
-                back_send[r * COLS + s * 2 + half] = packed_rows.astype(BF)
-
-    each(0, ROWS, product)
-
-    def push_back(t):
-        r, c = anyone(t)
-        push(BACK, back_send.at[r * COLS + c], back_got.at[me], (r, c))
-
-    each(1, ROWS * COLS, push_back)
+    def near(distance):
+        return lax.rem(row - distance + ROWS, ROWS)
+
+    def product(r, s):
+        full = nn(turned_left[r], tri_got[pl.ds(s * COLS, COLS)].reshape(512, 128))
+        parts = [full[g * 16 : (g + 1) * 16] for g in range(4)]
+        for half in range(2):
+            packed_rows = None
+            for g in range(4):
+                piece = roll(parts[g], g * 32 - 64 - half * 32)
+                packed_rows = piece if g == 0 else jnp.where(group == g, piece, packed_rows)
+            back_send[r * COLS + s * 2 + half] = packed_rows.astype(BF)
+
+    def push_back(r, c):
+        @pl.when(r * COLS + c != me)
+        def _():
+            push(BACK, back_send.at[r * COLS + c], back_got.at[me], (r, c))
+
+    for distance in range(ROWS):
+        new = near(distance)
+        arrived = tri_got.at[pl.ds(0, COLS - 1 if distance == 0 else COLS)]
+        pltpu.make_async_copy(arrived, arrived, tri_sem.at[new]).wait()
+        got = tri_got[pl.ds(new * COLS, COLS)].reshape(512, 128)
+        turned_left[new] = jnp.transpose(got.astype(F32))[:64].astype(BF)
+        product(new, new)
+        for older in range(distance):
+            product(new, near(older))
+            product(near(older), new)
+
+        def push_new(older):
+            push_back(new, near(older) * 2)
+            push_back(new, near(older) * 2 + 1)
+
+        def push_older(older):
+            push_back(near(older), new * 2)
+            push_back(near(older), new * 2 + 1)
+
+        each(0, distance + 1, push_new)
+        each(0, distance, push_older)
     back_got[me] = back_send[me]
     landed(BACK, back_got.at[pl.ds(0, ROWS * COLS - 1)])
 
@@ -358,6 +377,7 @@
             pltpu.VMEM((2, 8, 64, 512), BF),
             pltpu.VMEM((16, 128, 128), BF),
             pltpu.VMEM((16, 128, 128), BF),
+            pltpu.VMEM((8, 64, 512), BF),
             pltpu.VMEM((4, 512, 128), BF),
             pltpu.VMEM((4, 512, 128), BF),
             pltpu.VMEM((4, 512, 256), BF),
@@ -373,6 +393,7 @@
             pltpu.SemaphoreType.DMA((7,)),
             pltpu.SemaphoreType.DMA((8,)),
             pltpu.SemaphoreType.DMA((8,)),
+            pltpu.SemaphoreType.DMA((8,)),
         ],
         name="pairformer",
         compiler_params=pltpu.CompilerParams(

time: 87.5 us -> 85.1 us (0.973)
  Pallas kernels: 85 us -> 82.7 us
    pallas_call x1, Pallas kernels: 85 us -> 82.7 us  [on_device(): pl.pallas_call(block_kernel, out_shape=jax.ShapeDtypeStruct((64, 32, 128)...]
where the time goes in v5:
time: 85.1 us; the launch traced here: 85 us
  Pallas kernels  82.7 us (97%)
  local copies, waits for them, and re-layouts  2.26 us (3%)
    pallas_call x1, Pallas kernels, on_device(): pl.pallas_call(block_kernel, out_shape=jax.ShapeDtypeStruct((64, 32, 128)...  82.7 us
    unnamed x1, local copies, waits for them, and re-layouts  2.26 us

profile of v5, /device:TPU:105, one launch (start us, length us, event | category | flops | bytes accessed | tf_op | source)
XLA Modules:
  0.0 85.0 jit_solution(17349142679109125758)
XLA Ops:
  0.0 82.7 %pairformer.1 = f32[64,32,128]{2,1,0:T(8,128)} custom-call(s32[8]{0:T(128)} %lengths.1, f32[64,32,128]{2,1,0:T(8,128)} %pair_in.1, bf16[128,640]{1,0:T(8,128)(2,1)} %tri_in_in.1, bf16[128,128]{1,0:T(8,128)(2,1)} %tri_out_in.1, bf16[128,512]{1,0:T(8,128)(2,1)} %att_in_in.1, f32[4,128]{1,0:T(4,128)} %bitcast.1, bf16[128,128]{1,0:T(8,128)(2,1)} %att_out_in.1), custom_call_target="tpu_custom_call" | custom-call | tf_op jit(solution)/shard_map/pairformer/pallas_call | solution.py:356
  82.7 2.3 %copy.9 = f32[64,32,128]{2,1,0:T(8,128)} copy(f32[64,32,128]{2,1,0:T(8,128)} %pairformer.1) | data formatting | bytes 2097152

commit v6 on v5

--- a/solution.py
+++ b/solution.py
@@ -12,7 +12,7 @@
 COLS = 16
 BF = jnp.bfloat16
 F32 = jnp.float32
-TRI, BACK, NORM, BIAS_COL, BIAS_ROW, BIAS_TWIN, HEADS = range(7)
+TRI, BACK, NORM, NORM_TWIN, BIAS_COL, BIAS_ROW, HEADS = range(7)
 
 
 def layer_norm(values, axis):
@@ -50,10 +50,11 @@
     pair, tri_in, tri_out, att_in, att_bias, att_out,
     tri_send, tri_got, back_send, back_got, norm_send, norm_got,
     bias_send, bias_got, bias_rows, bias_all, head_send, head_got,
-    turned_left, queries, keys, values, wide, gate, gate2, pair1, packed, gate_packed, out_packed, load_sem, send_sem, recv_sem, tri_sem, row_sem, twin_sem,
+    turned_left, queries, keys, values, wide, gate, gate2, pair1, packed, gate_packed, out_packed, load_sem, send_sem, recv_sem, tri_sem, row_sem,
 ):
     row, col = lax.axis_index("row"), lax.axis_index("col")
     me = row * COLS + col
+    core = lax.rem(col, 2)
 
     loads = [
         pltpu.make_async_copy(src, dst, load_sem.at[n])
@@ -138,7 +139,7 @@
     for load in loads[2:]:
         load.wait()
     group = lane_group(128)
-    mine_first = jnp.where(col // 8 == 0, 1.0, 0.0)
+    mine_first = jnp.where(core == 0, 1.0, 0.0)
     for t in range(4):
         block = att_in[:, t * 128 : (t + 1) * 128].astype(F32)
         low = jnp.where(group < 2, block, 0.0)
@@ -230,61 +231,63 @@
 
     def push_bias_col(t):
         c = lax.rem(col + t, COLS)
-        push(BIAS_COL, bias_send.at[c // 8 * 2 + lax.rem(c, 2)], bias_got.at[col], (row, c))
+        heads = bias_send.at[pl.ds(lax.rem(c, 2) * 2, 2)]
+        push(BIAS_COL, heads, bias_got.at[col], (row, c))
 
     each(1, COLS, push_bias_col)
-    head = lax.rem(col, 2)
-    bias_got[col] = bias_send[col // 8 * 2 + head]
+    bias_got[col] = bias_send[pl.ds(core * 2, 2)]
 
     def push_norm(t):
-        c = lax.rem(col + t, COLS)
-        push(NORM, norm_send.at[lax.rem(c, 8)], norm_got.at[col], (row, c))
-
-    each(1, 5, push_norm)
+        g = lax.rem(col // 2 + t, 8)
+        push(NORM, norm_send.at[g], norm_got.at[core, col // 2], (row, g * 2 + core))
+
+    each(1, 4, push_norm)
+    norm_got[core, col // 2] = norm_send[col // 2]
 
     landed(BIAS_COL, bias_got.at[pl.ds(0, COLS - 1)])
-    for hi in range(4):
-        quads = []
-        for quad in range(4):
-            rows = None
-            for q in range(4):
-                piece = roll(bias_got[quad * 4 + q], q * 32 - hi * 32)
-                rows = piece if q == 0 else jnp.where(group == q, piece, rows)
-            length = jnp.where(lane < 64, lengths[quad * 2], lengths[quad * 2 + 1])
-            quads.append(jnp.where(lax.rem(lane, 64) < length, rows, -1000000000.0))
-        rows = jnp.concatenate(quads, 1)
-        top = jnp.max(rows, axis=1, keepdims=True)
-        bias_rows[hi * 16 : hi * 16 + 16] = (rows - top).astype(BF)
-    bias_all[head, row] = bias_rows[...]
+    for h in range(2):
+        for hi in range(4):
+            quads = []
+            for quad in range(4):
+                rows = None
+                for q in range(4):
+                    piece = roll(bias_got[quad * 4 + q, h], q * 32 - hi * 32)
+                    rows = piece if q == 0 else jnp.where(group == q, piece, rows)
+                length = jnp.where(lane < 64, lengths[quad * 2], lengths[quad * 2 + 1])
+                quads.append(jnp.where(lax.rem(lane, 64) < length, rows, -1000000000.0))
+            rows = jnp.concatenate(quads, 1)
+            top = jnp.max(rows, axis=1, keepdims=True)
+            bias_rows[h, hi * 16 : hi * 16 + 16] = (rows - top).astype(BF)
+    bias_all[row] = bias_rows[...]
+
+    def differ(a, b):
+        return a + b - 2 * a * b
+
+    def partner(t):
+        flip = 3 - (t - 1) // 2
+        low = differ(lax.rem(row, 2), flip % 2)
+        high = differ(lax.rem(row // 2, 2), flip // 2)
+        return low + 2 * high + 4 * differ(row // 4, 1 - t % 2 + t // 7)
 
     def push_bias_row(t):
-        r = lax.rem(row + t, ROWS)
-        push(BIAS_ROW, bias_rows, bias_all.at[head, row], (r, col), row_sem.at[row])
-
-    def push_twin(r):
-        twin = bias_all.at[head, r]
-        push(BIAS_TWIN, twin, twin, (row, col + 1 - 2 * head), twin_sem.at[r])
-
-    push_twin(row)
-
-    def push_both(t):
+        push(BIAS_ROW, bias_rows, bias_all.at[row], (partner(t), col), row_sem.at[row])
+
+    for t in range(1, 5):
         push_bias_row(t)
-        push_norm(2 * t + 3)
-        push_norm(2 * t + 4)
-
-    each(1, 6, push_both)
-    push_bias_row(6)
-    push_norm(15)
-    push_bias_row(7)
-    norm_got[col] = norm_send[lax.rem(col, 8)]
+        push_norm(t + 3)
+    for t in range(5, ROWS):
+        push_bias_row(t)
 
     for g in range(8):
         gate2[g] = sigmoid(nn(norm_send[g], gate_packed[...]))
 
-    landed(NORM, norm_got.at[pl.ds(0, COLS - 1)])
+    landed(NORM, norm_got.at[0, pl.ds(0, 7)])
+    twin = norm_got.at[core]
+    push(NORM_TWIN, twin, twin, (row, col + 1 - 2 * core))
+    landed(NORM_TWIN, norm_got.at[0])
     ones = jnp.ones((512, 128), BF)
     for n in range(4):
-        normed = norm_got[:, n * 32 : n * 32 + 32, :].reshape(512, 256)
+        normed = jnp.swapaxes(norm_got[:, :, n * 32 : n * 32 + 32, :], 0, 1).reshape(512, 256)
         queries[n] = (nn(normed, packed[:, 0:128]) * (DH ** (-0.5))).astype(BF)
         keys[n] = nn(normed, packed[:, 128:256]).astype(BF)
         values[n, :, 0:128] = nn(normed, packed[:, 256:384]).astype(BF)
@@ -293,13 +296,12 @@
     group = lane_group(64)
 
     def attend(r):
-        pltpu.make_async_copy(bias_rows, bias_rows, twin_sem.at[r]).wait()
         at = pl.ds(pl.multiple_of(r * 64, 64), 64)
 
         def pair_of_rows(n):
             query = queries[n, at, :]
             mine = [jnp.where(group == g, query, jnp.zeros_like(query)) for g in range(4)]
-            bias = [bias_all[0, r].astype(F32), bias_all[1, r].astype(F32)]
+            bias = [bias_all[r, 0].astype(F32), bias_all[r, 1].astype(F32)]
             score = nt(jnp.concatenate(mine, 0), keys[n]) + jnp.concatenate(bias + bias, 0)
             top = jnp.max(score, axis=1, keepdims=True)
             summed = nn(jnp.exp(score - top).astype(BF), values[n])
@@ -319,21 +321,19 @@
             def _():
                 push(HEADS, head_send.at[c], head_got.at[col], (row, c))
 
-    def attend_previous(t):
-        @pl.when(t < ROWS)
-        def _():
-            r = lax.rem(row - t + ROWS, ROWS)
-            pltpu.make_async_copy(bias_rows, bias_rows, row_sem.at[r]).wait()
-            push_twin(r)
-
-        attend(lax.rem(row - t + 1 + ROWS, ROWS))
-
-    each(1, ROWS + 1, attend_previous)
+    attend(row)
+
+    def attend_next(t):
+        r = partner(t)
+        pltpu.make_async_copy(bias_rows, bias_rows, row_sem.at[r]).wait()
+        attend(r)
+
+    each(1, ROWS, attend_next)
     head_got[col] = head_send[col]
     landed(HEADS, head_got.at[pl.ds(0, COLS - 1)])
 
     for g in range(8):
-        heads = jnp.concatenate([head_got[g], head_got[8 + g]], 1).astype(F32)
+        heads = jnp.concatenate([head_got[2 * g], head_got[2 * g + 1]], 1).astype(F32)
         result = nn((gate2[g] * heads).astype(BF), out_packed[...])
         for l in range(2):
             for hi in range(4):
@@ -344,10 +344,10 @@
 
     sent(TRI, tri_send.at[pl.ds(0, ROWS * COLS - 1)])
     sent(BACK, back_send.at[pl.ds(0, ROWS * COLS - 1)])
-    sent(NORM, norm_got.at[pl.ds(0, COLS - 1)])
+    sent(NORM, norm_got.at[0, pl.ds(0, 7)])
+    sent(NORM_TWIN, norm_got.at[0])
     sent(BIAS_COL, bias_got.at[pl.ds(0, COLS - 1)])
-    sent(BIAS_ROW, bias_all.at[0, pl.ds(0, ROWS - 1)])
-    sent(BIAS_TWIN, bias_all.at[0])
+    sent(BIAS_ROW, bias_all.at[pl.ds(0, ROWS - 1)])
     sent(HEADS, head_send.at[pl.ds(0, COLS - 1)])
 
 
@@ -370,11 +370,11 @@
             pltpu.VMEM((128, 16, 128), BF),
             pltpu.VMEM((128, 16, 128), BF),
             pltpu.VMEM((8, 128, 256), BF),
-            pltpu.VMEM((16, 128, 256), BF),
+            pltpu.VMEM((2, 8, 128, 256), BF),
             pltpu.VMEM((4, 16, 128), F32),
-            pltpu.VMEM((16, 16, 128), F32),
-            pltpu.VMEM((64, 512), BF),
-            pltpu.VMEM((2, 8, 64, 512), BF),
+            pltpu.VMEM((16, 2, 16, 128), F32),
+            pltpu.VMEM((2, 64, 512), BF),
+            pltpu.VMEM((8, 2, 64, 512), BF),
             pltpu.VMEM((16, 128, 128), BF),
             pltpu.VMEM((16, 128, 128), BF),
             pltpu.VMEM((8, 64, 512), BF),
@@ -393,7 +393,6 @@
             pltpu.SemaphoreType.DMA((7,)),
             pltpu.SemaphoreType.DMA((8,)),
             pltpu.SemaphoreType.DMA((8,)),
-            pltpu.SemaphoreType.DMA((8,)),
         ],
         name="pairformer",
         compiler_params=pltpu.CompilerParams(

time: 85.1 us -> 80.4 us (0.945)
  the two profiles are of different devices: /device:TPU:105 before, /device:TPU:9 now
where the time goes in v6:
time: 80.4 us; the launch traced here: 80.3 us
  Pallas kernels  78 us (97%)
  local copies, waits for them, and re-layouts  2.26 us (3%)
    pallas_call x1, Pallas kernels, on_device(): pl.pallas_call(block_kernel, out_shape=jax.ShapeDtypeStruct((64, 32, 128)...  78 us
    unnamed x1, local copies, waits for them, and re-layouts  2.26 us

profile of v6, /device:TPU:9, one launch (start us, length us, event | category | flops | bytes accessed | tf_op | source)
XLA Modules:
  0.0 80.3 jit_solution(9048602727682227495)
XLA Ops:
  0.0 78.0 %pairformer.1 = f32[64,32,128]{2,1,0:T(8,128)} custom-call(s32[8]{0:T(128)} %lengths.1, f32[64,32,128]{2,1,0:T(8,128)} %pair_in.1, bf16[128,640]{1,0:T(8,128)(2,1)} %tri_in_in.1, bf16[128,128]{1,0:T(8,128)(2,1)} %tri_out_in.1, bf16[128,512]{1,0:T(8,128)(2,1)} %att_in_in.1, f32[4,128]{1,0:T(4,128)} %bitcast.1, bf16[128,128]{1,0:T(8,128)(2,1)} %att_out_in.1), custom_call_target="tpu_custom_call" | custom-call | tf_op jit(solution)/shard_map/pairformer/pallas_call | solution.py:356
  78.0 2.3 %copy.9 = f32[64,32,128]{2,1,0:T(8,128)} copy(f32[64,32,128]{2,1,0:T(8,128)} %pairformer.1) | data formatting | bytes 2097152

commit v7 on v6

--- a/solution.py
+++ b/solution.py
@@ -50,7 +50,7 @@
     pair, tri_in, tri_out, att_in, att_bias, att_out,
     tri_send, tri_got, back_send, back_got, norm_send, norm_got,
     bias_send, bias_got, bias_rows, bias_all, head_send, head_got,
-    turned_left, queries, keys, values, wide, gate, gate2, pair1, packed, gate_packed, out_packed, load_sem, send_sem, recv_sem, tri_sem, row_sem,
+    turned_left, queries, keys, values, wide, gate, gate2, pair1, packed, gate_packed, out_packed, load_sem, send_sem, recv_sem, tri_sem, norm_sem, row_sem,
 ):
     row, col = lax.axis_index("row"), lax.axis_index("col")
     me = row * COLS + col
@@ -237,12 +237,27 @@
     each(1, COLS, push_bias_col)
     bias_got[col] = bias_send[pl.ds(core * 2, 2)]
 
+    def differ(a, b):
+        return a + b - 2 * a * b
+
+    chip = col // 2
+
+    def chip_partner(t):
+        flip = 8 - t
+        low = differ(lax.rem(chip, 2), flip % 2)
+        high = differ(lax.rem(chip // 2, 2), flip // 2 % 2)
+        return low + 2 * high + 4 * differ(chip // 4, flip // 4)
+
     def push_norm(t):
-        g = lax.rem(col // 2 + t, 8)
-        push(NORM, norm_send.at[g], norm_got.at[core, col // 2], (row, g * 2 + core))
-
-    each(1, 4, push_norm)
-    norm_got[core, col // 2] = norm_send[col // 2]
+        g = chip_partner(t)
+        push(NORM, norm_send.at[g], norm_got.at[core, chip], (row, g * 2 + core), norm_sem.at[chip])
+
+    def push_twin(g):
+        twin = norm_got.at[core, g]
+        push(NORM_TWIN, twin, twin, (row, col + 1 - 2 * core))
+
+    each(1, 8, push_norm)
+    norm_got[core, chip] = norm_send[chip]
 
     landed(BIAS_COL, bias_got.at[pl.ds(0, COLS - 1)])
     for h in range(2):
@@ -260,30 +275,28 @@
             bias_rows[h, hi * 16 : hi * 16 + 16] = (rows - top).astype(BF)
     bias_all[row] = bias_rows[...]
 
-    def differ(a, b):
-        return a + b - 2 * a * b
-
-    def partner(t):
+    def partner(step):
+        t = lax.rem(step - 1 + chip, 7) + 1
         flip = 3 - (t - 1) // 2
-        low = differ(lax.rem(row, 2), flip % 2)
+        low = differ(lax.rem(row, 2), lax.rem(flip, 2))
         high = differ(lax.rem(row // 2, 2), flip // 2)
-        return low + 2 * high + 4 * differ(row // 4, 1 - t % 2 + t // 7)
+        return low + 2 * high + 4 * differ(row // 4, 1 - lax.rem(t, 2) + t // 7)
 
     def push_bias_row(t):
         push(BIAS_ROW, bias_rows, bias_all.at[row], (partner(t), col), row_sem.at[row])
 
-    for t in range(1, 5):
-        push_bias_row(t)
-        push_norm(t + 3)
-    for t in range(5, ROWS):
-        push_bias_row(t)
+    push_twin(chip)
+    each(1, ROWS, push_bias_row)
 
     for g in range(8):
         gate2[g] = sigmoid(nn(norm_send[g], gate_packed[...]))
 
-    landed(NORM, norm_got.at[0, pl.ds(0, 7)])
-    twin = norm_got.at[core]
-    push(NORM_TWIN, twin, twin, (row, col + 1 - 2 * core))
+    def hand_over(t):
+        g = chip_partner(t)
+        pltpu.make_async_copy(norm_got.at[0, 0], norm_got.at[0, 0], norm_sem.at[g]).wait()
+        push_twin(g)
+
+    each(1, 8, hand_over)
     landed(NORM_TWIN, norm_got.at[0])
     ones = jnp.ones((512, 128), BF)
     for n in range(4):
@@ -393,6 +406,7 @@
             pltpu.SemaphoreType.DMA((7,)),
             pltpu.SemaphoreType.DMA((8,)),
             pltpu.SemaphoreType.DMA((8,)),
+            pltpu.SemaphoreType.DMA((8,)),
         ],
         name="pairformer",
         compiler_params=pltpu.CompilerParams(

time: 80.4 us -> 79.4 us (0.988)
  the two profiles are of different devices: /device:TPU:9 before, /device:TPU:11 now
where the time goes in v7:
time: 79.4 us; the launch traced here: 79.2 us
  Pallas kernels  77 us (97%)
  local copies, waits for them, and re-layouts  2.26 us (3%)
    pallas_call x1, Pallas kernels, on_device(): pl.pallas_call(block_kernel, out_shape=jax.ShapeDtypeStruct((64, 32, 128)...  77 us
    unnamed x1, local copies, waits for them, and re-layouts  2.26 us

profile of v7, /device:TPU:11, one launch (start us, length us, event | category | flops | bytes accessed | tf_op | source)
XLA Modules:
  0.0 79.2 jit_solution(18146256380068192534)
XLA Ops:
  0.0 77.0 %pairformer.1 = f32[64,32,128]{2,1,0:T(8,128)} custom-call(s32[8]{0:T(128)} %lengths.1, f32[64,32,128]{2,1,0:T(8,128)} %pair_in.1, bf16[128,640]{1,0:T(8,128)(2,1)} %tri_in_in.1, bf16[128,128]{1,0:T(8,128)(2,1)} %tri_out_in.1, bf16[128,512]{1,0:T(8,128)(2,1)} %att_in_in.1, f32[4,128]{1,0:T(4,128)} %bitcast.1, bf16[128,128]{1,0:T(8,128)(2,1)} %att_out_in.1), custom_call_target="tpu_custom_call" | custom-call | tf_op jit(solution)/shard_map/pairformer/pallas_call | solution.py:369
  77.0 2.3 %copy.9 = f32[64,32,128]{2,1,0:T(8,128)} copy(f32[64,32,128]{2,1,0:T(8,128)} %pairformer.1) | data formatting | bytes 2097152

commit v8 on v7

--- a/solution.py
+++ b/solution.py
@@ -164,7 +164,9 @@
     for _ in range(3):
         part = rest.astype(BF)
         rest = rest - part.astype(F32)
-        bias_weights.append(part)
+        bias_weights += [part.astype(F32), jnp.zeros((4, 128), F32)]
+
+    bias_weights = jnp.concatenate(bias_weights, 0).astype(BF)
 
     group = lane_group(16)
 
@@ -224,8 +226,8 @@
             norm_send[lo // 2, at : at + 32, (hi % 2) * 128 : (hi % 2) * 128 + 128] = block
             blocks.append(block)
         stacked = jnp.concatenate(blocks, 0)
-        parts = [nt(w, stacked) for w in bias_weights]
-        bias = parts[0] + (parts[1] + parts[2])
+        parts = nt(bias_weights, stacked)
+        bias = parts[0:4] + (parts[8:12] + parts[16:20])
         for h in range(H):
             bias_send[h, lo : lo + 1, :] = bias[h : h + 1]
 

time: 79.4 us -> 78.6 us (0.990)
  Pallas kernels: 77 us -> 76.2 us
where the time goes in v8:
time: 78.6 us; the launch traced here: 78.5 us
  Pallas kernels  76.2 us (97%)
  local copies, waits for them, and re-layouts  2.26 us (3%)
    pallas_call x1, Pallas kernels, on_device(): pl.pallas_call(block_kernel, out_shape=jax.ShapeDtypeStruct((64, 32, 128)...  76.2 us
    unnamed x1, local copies, waits for them, and re-layouts  2.26 us

profile of v8, /device:TPU:11, one launch (start us, length us, event | category | flops | bytes accessed | tf_op | source)
XLA Modules:
  0.0 78.5 jit_solution(141135874046242002)
XLA Ops:
  0.0 76.2 %pairformer.1 = f32[64,32,128]{2,1,0:T(8,128)} custom-call(s32[8]{0:T(128)} %lengths.1, f32[64,32,128]{2,1,0:T(8,128)} %pair_in.1, bf16[128,640]{1,0:T(8,128)(2,1)} %tri_in_in.1, bf16[128,128]{1,0:T(8,128)(2,1)} %tri_out_in.1, bf16[128,512]{1,0:T(8,128)(2,1)} %att_in_in.1, f32[4,128]{1,0:T(4,128)} %bitcast.1, bf16[128,128]{1,0:T(8,128)(2,1)} %att_out_in.1), custom_call_target="tpu_custom_call" | custom-call | tf_op jit(solution)/shard_map/pairformer/pallas_call | solution.py:371
  76.2 2.3 %copy.9 = f32[64,32,128]{2,1,0:T(8,128)} copy(f32[64,32,128]{2,1,0:T(8,128)} %pairformer.1) | data formatting | bytes 2097152
